TPU v7x, 32 devices: a whole 2x2x4 slice. The times are simulated.
32 devices in a mesh: head: 4 (over y, core), shard: 8 (over z, x).
Axes of the slice: x: 2, y: 2, z: 4, core: 2. Of those that a mesh axis runs over, the one named last changes fastest.
Arguments:
- layer_input: float32 [16384, 1536], P(('shard', 'head')), may hold values from -6 to 6
- cotangent: float32 [16384, 1536], P(('shard', 'head')), may hold values from -6 to 6
- weight_in: float32 [1536, 6448], P('shard'), may hold values from -0.15625 to 0.15625
- first_in: float32 [1536, 6448], P('shard'), may hold values from -24 to 24
- second_in: float32 [1536, 6448], P('shard'), may hold values from 77.0048 to 311.296
- weight_out: float32 [3072, 1536], P('shard'), may hold values from -0.109375 to 0.109375
- first_out: float32 [3072, 1536], P('shard'), may hold values from -80 to 80
- second_out: float32 [3072, 1536], P('shard'), may hold values from 861.7984 to 3440.64
- small_params: float32 [21392], P('shard'), as said below
- first_small: float32 [21392], P('shard'), may hold values from -64 to 64
- second_small: float32 [21392], P('shard'), may hold values from 8.192 to 4259.84
Outputs:
- out: float32 [16384, 1536], P(('shard', 'head'))
- d_input: float32 [16384, 1536], P(('shard', 'head'))
- new_first_in: float32 [1536, 6448], P('shard')
- new_second_in: float32 [1536, 6448], P('shard')
- new_weight_in: float32 [1536, 6448], P('shard')
- new_first_out: float32 [3072, 1536], P('shard')
- new_second_out: float32 [3072, 1536], P('shard')
- new_weight_out: float32 [3072, 1536], P('shard')
- new_first_small: float32 [21392], P('shard')
- new_second_small: float32 [21392], P('shard')
- new_small: float32 [21392], P('shard')
Inputs may be any that keep to these rules, and one draw needn't show every extreme that they name: `small_params`: packed as stated; every step offset lies in [-10, -3].
All inputs are finite; a program needn't handle non-finite values.
Results may differ from a plain program's by a relative error of at most 0.0019.
The roundings to bfloat16 on the way count: a program that leaves them out, or rounds other values in their place, can miss the bound.
Values may be sent and summed in bfloat16 or wider, within the bound.
A program may use at most 320 MiB of HBM per device.

v0:
```python
import jax
import jax.numpy as jnp
from jax import lax
from jax.sharding import PartitionSpec as P

D = 1536
DI = 3072
HEADS = 48
HEADDIM = 64
NSTATE = 128
CONV = 4
BLOCK = 256
SEQS = 1
STEP = 5
XBC = 3328


EPSILON = 1e-05
BETA_FIRST = 0.9
BETA_SECOND = 0.95
ADAM_EPSILON = 1e-08
RATE_MATRIX = 0.02
RATE_SMALL = 0.2
DECAY_MATRIX = 0.1
HIGHEST = lax.Precision.HIGHEST


def from_behind(shard, axis, by):
    peers = lax.axis_size(axis)
    pairs = [(i, i + by) for i in range(peers) if 0 <= i + by < peers]
    return lax.ppermute(shard, axis, pairs)


def prefix(value, axis, join, neutral, backward):
    count, mine = (lax.axis_size(axis), lax.axis_index(axis))
    pieces = jax.tree.map(lambda part: lax.all_gather(part, axis), value)
    if backward:
        pieces = jax.tree.map(lambda part: part[::-1], pieces)
        mine = count - 1 - mine
    total = jax.tree.map(
        lambda part, zero: jnp.full_like(part, 0) + jnp.asarray(zero, part.dtype), value, neutral
    )

    def step(position, total):
        longer = join(total, jax.tree.map(lambda part: part[position], pieces))
        return jax.tree.map(lambda new, old: jnp.where(position < mine, new, old), longer, total)

    return lax.fori_loop(0, count - 1, step, total)


def shortened(shard):
    return jax.tree.map(lambda a: a.astype(jnp.bfloat16) if a.dtype == jnp.float32 else a, shard)


def unpack(packed):
    offset = 0
    conv_weight = packed[offset : offset + CONV * XBC].reshape(CONV, XBC)
    offset = offset + CONV * XBC
    conv_bias = packed[offset : offset + XBC]
    offset = offset + XBC
    dt_bias = packed[offset : offset + HEADS]
    a_log = packed[offset + HEADS : offset + 2 * HEADS]
    skip_gain = packed[offset + 2 * HEADS : offset + 3 * HEADS]
    offset = offset + 3 * HEADS
    norm_gain = packed[offset : offset + DI]
    pre_gain = packed[offset + DI : offset + DI + D]
    return (conv_weight, conv_bias, dt_bias, a_log, skip_gain, norm_gain, pre_gain)


def adamw(weight, moment_one, moment_two, gradient, step_rate, weight_decay):
    moment_one = BETA_FIRST * moment_one + (1.0 - BETA_FIRST) * gradient
    moment_two = BETA_SECOND * moment_two + (1.0 - BETA_SECOND) * gradient * gradient
    first_hat = moment_one / (1.0 - BETA_FIRST**STEP)
    second_hat = moment_two / (1.0 - BETA_SECOND**STEP)
    weight = weight - step_rate * (
        first_hat / (jnp.sqrt(second_hat) + ADAM_EPSILON) + weight_decay * weight
    )
    return (moment_one, moment_two, weight)


def forward_combine(earlier, later):
    return (earlier[0] * later[0], earlier[1] * later[0][:, None, None] + later[1])


def backward_combine(earlier, later):
    return (earlier[0] * later[0], later[1] + later[0][:, None, None] * earlier[1])


def place_heads(values, head_start):
    return lax.dynamic_update_slice_in_dim(jnp.zeros((HEADS,), jnp.float32), values, head_start, 0)


def per_device(
    layer_input,
    cotangent,
    weight_in,
    first_in,
    second_in,
    weight_out,
    first_out,
    second_out,
    small_params,
    first_small,
    second_small,
):
    head_count = lax.axis_size("head")
    shard_count = lax.axis_size("shard")
    tok_rows = layer_input.shape[0]
    group_rows = head_count * tok_rows
    local_heads = HEADS // head_count
    head_width = DI // head_count
    block_count = group_rows // BLOCK
    rim_count = CONV - 1
    head_index = lax.axis_index("head")
    shard_index = lax.axis_index("shard")
    seq_length = group_rows * shard_count // SEQS
    seq_start = shard_index * group_rows % seq_length == 0
    seq_end = (shard_index + 1) * group_rows % seq_length == 0
    chan_start = head_index * head_width
    head_start = head_index * local_heads
    full_in, full_out, full_small = (
        lax.all_gather(weight_in.astype(jnp.bfloat16), "shard", axis=0, tiled=True),
        lax.all_gather(weight_out.astype(jnp.bfloat16), "shard", axis=0, tiled=True),
        lax.all_gather(small_params.astype(jnp.bfloat16), "shard", axis=0, tiled=True),
    )
    conv_weight, conv_bias, dt_bias, a_log, skip_all, norm_gain, pre_gain = unpack(
        full_small.astype(jnp.float32)
    )
    inv_scale = lax.rsqrt(jnp.mean(layer_input * layer_input, axis=-1, keepdims=True) + EPSILON)
    unit_input = layer_input * inv_scale
    normed = (unit_input * pre_gain).astype(jnp.bfloat16)
    projected = jnp.dot(normed, full_in, preferred_element_type=jnp.float32).astype(jnp.bfloat16)
    gate_raw = projected[:, :DI].astype(jnp.float32)
    x_send = projected[:, DI : 2 * DI].reshape(tok_rows, head_count, head_width)
    bc_part = projected[:, 2 * DI : DI + XBC]
    dt_send = projected[:, DI + XBC :].reshape(tok_rows, head_count, local_heads)
    x_recv, dt_recv = (
        lax.all_to_all(x_send, "head", split_axis=1, concat_axis=0, tiled=True),
        lax.all_to_all(dt_send, "head", split_axis=1, concat_axis=0, tiled=True),
    )
    x_local = x_recv[:, 0]
    bc_local = lax.all_gather(bc_part, "head", axis=0, tiled=True)
    conv_cols = jnp.concatenate(
        [lax.dynamic_slice_in_dim(conv_weight, chan_start, head_width, 1), conv_weight[:, DI:]],
        axis=1,
    )
    conv_offset = jnp.concatenate(
        [lax.dynamic_slice_in_dim(conv_bias, chan_start, head_width, 0), conv_bias[DI:]]
    )
    before_conv = jnp.concatenate([x_local, bc_local], axis=1)
    rim_rows = from_behind(before_conv[group_rows - rim_count :], "shard", 1)
    rim_rows = jnp.where(seq_start, jnp.zeros_like(rim_rows), rim_rows)
    padded = jnp.concatenate([rim_rows, before_conv], axis=0).astype(jnp.float32)
    conv_out = conv_offset + sum(
        (conv_cols[tap] * padded[tap : tap + group_rows] for tap in range(CONV))
    )
    activated = jax.nn.silu(conv_out)
    x_heads = activated[:, :head_width].reshape(block_count, BLOCK, local_heads, HEADDIM)
    b_rows = activated[:, head_width : head_width + NSTATE].reshape(block_count, BLOCK, NSTATE)
    c_rows = activated[:, head_width + NSTATE :].reshape(block_count, BLOCK, NSTATE)
    offset_heads = lax.dynamic_slice_in_dim(dt_bias, head_start, local_heads)
    decay_rate = -jnp.exp(lax.dynamic_slice_in_dim(a_log, head_start, local_heads))
    skip_gain = lax.dynamic_slice_in_dim(skip_all, head_start, local_heads)
    pre_step = dt_recv.reshape(block_count, BLOCK, local_heads).astype(jnp.float32) + offset_heads
    step_size = jax.nn.softplus(pre_step)
    log_decay = jnp.cumsum(step_size * decay_rate, axis=1)
    block_total = log_decay[:, -1]
    decay_cols = jnp.swapaxes(log_decay, 1, 2)
    step_cols = jnp.swapaxes(step_size, 1, 2)
    causal = jnp.arange(BLOCK)[:, None] >= jnp.arange(BLOCK)[None, :]
    spread = decay_cols[:, :, :, None] - decay_cols[:, :, None, :]
    weight = jnp.exp(jnp.where(causal, spread, -jnp.inf))
    scores = jnp.einsum("ctn,csn->cts", c_rows, b_rows, precision=HIGHEST)
    mixing = weight * scores[:, None]
    y_diag = jnp.einsum(
        "chts,cshp->cthp", mixing * step_cols[:, :, None, :], x_heads, precision=HIGHEST
    )
    tail_decay = jnp.exp(block_total[:, None, :] - log_decay)
    weighted = x_heads * (tail_decay * step_size)[..., None]
    block_states = jnp.einsum("cshp,csn->chpn", weighted, b_rows, precision=HIGHEST)
    inclusive = jnp.cumsum(block_total, axis=0)
    exclusive = inclusive - block_total
    overall = inclusive[-1]
    block_ids = jnp.arange(block_count)
    later_mask = block_ids[:, None] > block_ids[None, :]
    carry_in = jnp.exp(
        jnp.where(later_mask[None], exclusive.T[:, :, None] - inclusive.T[:, None, :], -jnp.inf)
    )
    local_in = jnp.einsum("hcd,dhpn->chpn", carry_in, block_states, precision=HIGHEST)
    dev_state = jnp.einsum(
        "ch,chpn->hpn", jnp.exp(overall[None] - inclusive), block_states, precision=HIGHEST
    )
    dev_decay = jnp.where(seq_start, 0.0, jnp.exp(overall))
    prior_decay, prior_state = prefix(
        (dev_decay, dev_state),
        "shard",
        forward_combine,
        (jnp.ones_like(dev_decay), jnp.zeros_like(dev_state)),
        False,
    )
    prior_state = jnp.where(seq_start, 0.0, prior_state)
    state_in = local_in + jnp.exp(exclusive)[:, :, None, None] * prior_state[None]
    y_off = (
        jnp.einsum("chpn,ctn->cthp", state_in, c_rows, precision=HIGHEST)
        * jnp.exp(log_decay)[..., None]
    )
    y_ssm = y_diag + y_off
    y_all = y_ssm + skip_gain[:, None] * x_heads
    y_send = y_all.reshape(group_rows, 1, head_width).astype(jnp.bfloat16)
    y_tokens = (
        lax.all_to_all(y_send, "head", split_axis=0, concat_axis=1, tiled=True)
        .reshape(tok_rows, DI)
        .astype(jnp.float32)
    )
    gate_sigmoid = jax.nn.sigmoid(gate_raw)
    gate_silu = gate_raw * gate_sigmoid
    gated = y_tokens * gate_silu
    gate_scale = lax.rsqrt(jnp.mean(gated * gated, axis=-1, keepdims=True) + EPSILON)
    unit_gated = gated * gate_scale
    mixed = (unit_gated * norm_gain).astype(jnp.bfloat16)
    result = layer_input + jnp.dot(mixed, full_out, preferred_element_type=jnp.float32)
    cot_low = cotangent.astype(jnp.bfloat16)
    d_mixed = jnp.einsum("td,id->ti", cot_low, full_out, preferred_element_type=jnp.float32)
    grad_out = jnp.einsum("ti,td->id", mixed, cot_low, preferred_element_type=jnp.float32)
    grad_norm_gain = jnp.sum(d_mixed * unit_gated, axis=0)
    d_unit = d_mixed * norm_gain
    d_gated = gate_scale * (
        d_unit - unit_gated * jnp.mean(d_unit * unit_gated, axis=-1, keepdims=True)
    )
    d_y = d_gated * gate_silu
    d_gate = d_gated * y_tokens * gate_sigmoid * (1.0 + gate_raw * (1.0 - gate_sigmoid))
    d_heads = lax.all_to_all(
        d_y.reshape(tok_rows, head_count, head_width),
        "head",
        split_axis=1,
        concat_axis=0,
        tiled=True,
    )
    dy_heads = d_heads.reshape(block_count, BLOCK, local_heads, HEADDIM)
    grad_skip = jnp.sum(dy_heads * x_heads, axis=(0, 1, 3))
    scaled_dy = dy_heads * jnp.exp(log_decay)[..., None]
    block_grads = jnp.einsum("cthp,ctn->chpn", scaled_dy, c_rows, precision=HIGHEST)
    dev_grad = jnp.einsum("ch,chpn->hpn", jnp.exp(exclusive), block_grads, precision=HIGHEST)
    back_decay = jnp.where(seq_end, 0.0, jnp.exp(overall))
    after_decay, after_grad = prefix(
        (back_decay, dev_grad),
        "shard",
        backward_combine,
        (jnp.ones_like(back_decay), jnp.zeros_like(dev_grad)),
        True,
    )
    after_grad = jnp.where(seq_end, 0.0, after_grad)
    earlier_mask = block_ids[:, None] < block_ids[None, :]
    carry_back = jnp.exp(
        jnp.where(earlier_mask[None], exclusive.T[:, None, :] - inclusive.T[:, :, None], -jnp.inf)
    )
    grad_end = (
        jnp.einsum("hcd,dhpn->chpn", carry_back, block_grads, precision=HIGHEST)
        + jnp.exp(overall[None] - inclusive)[:, :, None, None] * after_grad[None]
    )
    q_intra = jnp.einsum("chts,cthp->cshp", mixing, dy_heads, precision=HIGHEST)
    q_off = (
        jnp.einsum("chpn,csn->cshp", grad_end, b_rows, precision=HIGHEST) * tail_decay[..., None]
    )
    q_all = q_intra + q_off
    dx_ssd = q_all * step_size[..., None]
    pair_grad = (
        jnp.einsum("cthp,cshp->chts", dy_heads, x_heads, precision=HIGHEST)
        * weight
        * step_cols[:, :, None, :]
    )
    d_brows = jnp.einsum("chts,ctn->csn", pair_grad, c_rows, precision=HIGHEST) + jnp.einsum(
        "cshp,chpn->csn", weighted, grad_end, precision=HIGHEST
    )
    d_crows = jnp.einsum("chts,csn->ctn", pair_grad, b_rows, precision=HIGHEST) + jnp.einsum(
        "cthp,chpn->ctn", scaled_dy, state_in, precision=HIGHEST
    )
    d_lam = jnp.sum(dy_heads * y_ssm, axis=-1) - jnp.sum(x_heads * dx_ssd, axis=-1)
    state_end = state_in * jnp.exp(block_total)[:, :, None, None] + block_states
    tail_sum = jnp.sum(grad_end * state_end, axis=(2, 3))
    d_logdecay = jnp.flip(jnp.cumsum(jnp.flip(d_lam, 1), axis=1), 1) + tail_sum[:, None, :]
    d_step = jnp.sum(x_heads * q_all, axis=-1) + d_logdecay * decay_rate
    grad_alog = jnp.sum(d_logdecay * step_size, axis=(0, 1)) * decay_rate
    d_dtpre = d_step * jax.nn.sigmoid(pre_step)
    grad_dtb = jnp.sum(d_dtpre, axis=(0, 1))
    dx_all = dx_ssd + skip_gain[:, None] * dy_heads
    d_act = jnp.concatenate(
        [
            dx_all.reshape(group_rows, head_width),
            d_brows.reshape(group_rows, NSTATE),
            d_crows.reshape(group_rows, NSTATE),
        ],
        axis=1,
    )
    conv_sigmoid = jax.nn.sigmoid(conv_out)
    d_conv = d_act * conv_sigmoid * (1.0 + conv_out * (1.0 - conv_sigmoid))
    grad_convw = jnp.stack(
        [jnp.sum(d_conv * padded[tap : tap + group_rows], axis=0) for tap in range(CONV)]
    )
    grad_convb = jnp.sum(d_conv, axis=0)
    d_padded = sum(
        (jnp.pad(d_conv * conv_cols[tap], ((tap, CONV - 1 - tap), (0, 0))) for tap in range(CONV))
    )
    d_rim = jnp.where(seq_start, 0.0, d_padded[:rim_count])
    from_next = from_behind(d_rim, "shard", -1)
    d_inputs = d_padded[rim_count:]
    d_inputs = jnp.concatenate(
        [d_inputs[: group_rows - rim_count], d_inputs[group_rows - rim_count :] + from_next], axis=0
    )
    dx_send = d_inputs[:, :head_width]
    dx_back, dt_back = (
        lax.all_to_all(
            shortened(dx_send.reshape(group_rows, 1, dx_send.shape[1])),
            "head",
            split_axis=0,
            concat_axis=1,
            tiled=True,
        ),
        lax.all_to_all(
            shortened(d_dtpre.reshape(group_rows, 1, local_heads)),
            "head",
            split_axis=0,
            concat_axis=1,
            tiled=True,
        ),
    )
    d_bc = lax.psum_scatter(d_inputs[:, head_width:], "head", scatter_dimension=0, tiled=True)
    dx_tokens = dx_back.reshape(tok_rows, DI)
    d_proj = jnp.concatenate(
        [d_gate, dx_tokens, d_bc, dt_back.reshape(tok_rows, HEADS)], axis=1
    ).astype(jnp.bfloat16)
    d_normed = jnp.einsum("tf,df->td", d_proj, full_in, preferred_element_type=jnp.float32)
    grad_in = jnp.einsum("td,tf->df", normed, d_proj, preferred_element_type=jnp.float32)
    grad_pre_gain = jnp.sum(d_normed * unit_input, axis=0)
    d_hat = d_normed * pre_gain
    d_input = cotangent + inv_scale * (
        d_hat - unit_input * jnp.mean(d_hat * unit_input, axis=-1, keepdims=True)
    )
    conv_x_grad = lax.dynamic_update_slice_in_dim(
        jnp.zeros((CONV, DI), jnp.float32), grad_convw[:, :head_width], chan_start, 1
    )
    conv_w_full = jnp.concatenate([conv_x_grad, grad_convw[:, head_width:]], axis=1).reshape(-1)
    conv_b_full = jnp.concatenate(
        [
            lax.dynamic_update_slice_in_dim(
                jnp.zeros((DI,), jnp.float32), grad_convb[:head_width], chan_start, 0
            ),
            grad_convb[head_width:],
        ]
    )
    grad_small = jnp.concatenate(
        [
            conv_w_full,
            conv_b_full,
            place_heads(grad_dtb, head_start),
            place_heads(grad_alog, head_start),
            place_heads(grad_skip, head_start),
            grad_norm_gain,
            grad_pre_gain,
        ]
    )
    part_in, part_out, part_small = (
        lax.psum_scatter(grad_in, "shard", scatter_dimension=0, tiled=True),
        lax.psum_scatter(grad_out, "shard", scatter_dimension=0, tiled=True),
        lax.psum_scatter(grad_small, "shard", scatter_dimension=0, tiled=True),
    )
    total_in, total_out, total_small = lax.psum((part_in, part_out, part_small), "head")
    one_in, two_in, new_in = adamw(
        weight_in, first_in, second_in, total_in, RATE_MATRIX, DECAY_MATRIX
    )
    one_out, two_out, new_out = adamw(
        weight_out, first_out, second_out, total_out, RATE_MATRIX, DECAY_MATRIX
    )
    one_small, two_small, new_small = adamw(
        small_params, first_small, second_small, total_small, RATE_SMALL, 0.0
    )
    return (
        result,
        d_input,
        one_in,
        two_in,
        new_in,
        one_out,
        two_out,
        new_out,
        one_small,
        two_small,
        new_small,
    )


def solution(mesh):
    placed = (
        P(("shard", "head"), None),
        P(("shard", "head"), None),
        P("shard", None),
        P("shard", None),
        P("shard", None),
        P("shard", None),
        P("shard", None),
        P("shard", None),
        P("shard"),
        P("shard"),
        P("shard"),
    )
    return jax.shard_map(
        per_device,
        mesh=mesh,
        in_specs=placed,
        out_specs=(
            P(("shard", "head"), None),
            P(("shard", "head"), None),
            P("shard", None),
            P("shard", None),
            P("shard", None),
            P("shard", None),
            P("shard", None),
            P("shard", None),
            P("shard"),
            P("shard"),
            P("shard"),
        ),
        check_vma=False,
    )
```

profile of v0, /device:TPU:0, one launch (start us, length us, event | category | flops | bytes accessed | tf_op | source)
XLA Modules:
  0.0 2321.7 jit_solution(10372394547104301125)
XLA Ops:
  13.3 69.3 %all-reduce.4 = bf16[21392]{0:T(1024)(128)(2,1)S(1)} all-reduce(bf16[21392]{0:T(1024)(128)(2,1)S(1)} %dynamic-update-slice), channel_id=1, replica_groups=mesh['head'=4,'shard'=8] {'shard'}, use_global_device_ids=true, to_apply=%add.4 | all-reduce | flops 21392 | bytes 85568
  82.9 318.3 %all-gather.10.cloned.1.call-done = bf16[1536,6448]{1,0:T(8,128)(2,1)} async-done(((bf16[192,6448]{1,0:T(8,128)(2,1)}), bf16[1536,6448]{1,0:T(8,128)(2,1)}) %all-gather.10.cloned.1.call-update) | async-done | bytes 19808272 | tf_op jit(solution)/shard_map/all_gather | solution.py:122
  401.2 17.1 convolution_convert_fusion
  443.5 29.9 %all-to-all-done = bf16[512,4,768]{0,2,1:T(8,128)(2,1)S(1)} async-done(((bf16[512,4,768]{0,2,1:T(8,128)(2,1)}), bf16[512,4,768]{0,2,1:T(8,128)(2,1)S(1)}, u32[]{:S(2)}, u32[]{:S(2)}) %all-to-all-start) | async-done | bytes 3145760 | tf_op jit(solution)/shard_map/all_to_all | solution.py:138
  513.2 11.1 fusion.37
  534.2 21.3 all-gather.2
  576.2 31.2 %fusion.2 = f32[8,12,64,256]{3,2,1,0:T(8,128)} fusion(f32[8,12,256]{2,1,0:T(8,128)S(1)} %copy-done.48, f32[8,256,256]{2,1,0:T(8,128)S(1)} %fusion.139, f32[8,12,256]{2,1,0:T(8,128)S(1)} %copy-done.47, pred[256,256]{1,0:T(8,128)(4,1)S(1)} %iota_compare_fusion, f32[8,256,12,64]{1,0,3,2:T(8,128)S(1)} %bitcast.230), kind=kOutput, calls=%fused_computation.7 | convolution fusion | flops 4857004032 | bytes 14942208 | tf_op jit(solution)/shard_map/chts,cshp->cthp/dot_general | solution.py:175
  615.6 13.8 add_convert_fusion
  659.9 36.2 %all-to-all-done.2 = bf16[4,2,196608]{2,1,0:T(2,128)(2,1)} async-done(((bf16[4,2,196608]{2,1,0:T(2,128)(2,1)}), bf16[4,2,196608]{2,1,0:T(2,128)(2,1)}, u32[]{:S(2)}, u32[]{:S(2)}) %all-to-all-start.2) | async-done | bytes 3145760 | tf_op jit(solution)/shard_map/all_to_all | solution.py:211
  722.1 10.9 all-gather.14.cloned.1.call-done
  732.9 13.2 multiply_reduce_fusion.5
  759.1 70.6 %all-to-all-done.3 = f32[512,4,768]{0,2,1:T(8,128)} async-done(((f32[512,4,768]{0,2,1:T(8,128)}), f32[512,4,768]{0,2,1:T(8,128)}, u32[]{:S(2)}, u32[]{:S(2)}) %all-to-all-start.3) | async-done | bytes 6291488 | tf_op jit(solution)/shard_map/all_to_all | solution.py:232
  864.7 17.5 all-gather.3
  882.7 15.9 fusion.74
  898.7 31.5 %multiply_reduce_fusion = f32[8,256,256]{2,1,0:T(8,128)S(1)} fusion(f32[8,12,256]{2,1,0:T(8,128)S(1)} %copy-done.48, f32[8,12,256]{2,1,0:T(8,128)S(1)} %copy-done.47, pred[256,256]{1,0:T(8,128)(4,1)S(1)} %iota_compare_fusion, f32[8,256,12,64]{1,0,3,2:T(8,128)} %reshape.280, f32[8,256,12,64]{1,0,3,2:T(8,128)S(1)} %bitcast.233), kind=kOutput, calls=%fused_computation.6 | convolution fusion | flops 4862771200 | bytes 14942208 | tf_op jit(solution)/shard_map/cthp,cshp->chts/dot_general | solution.py:268
  939.9 26.4 %fusion.5 = f32[8,12,64,256]{3,2,1,0:T(8,128)} fusion(f32[8,256,256]{2,1,0:T(8,128)} %copy-done.33, f32[8,12,256]{2,1,0:T(8,128)} %copy-done.46, pred[256,256]{1,0:T(8,128)(4,1)S(1)} %copy-done.52, f32[8,256,12,64]{1,0,3,2:T(8,128)} %reshape.280), kind=kOutput, calls=%fused_computation.11 | convolution fusion | flops 4850712576 | bytes 14843904 | tf_op jit(solution)/shard_map/chts,cthp->cshp/dot_general | solution.py:261
  970.4 16.3 while.29
  988.5 15.0 fusion.71
  1010.5 16.8 multiply_reduce_fusion.6
  1035.0 14.9 multiply_reduce_fusion.4
  1049.9 12.0 broadcast_multiply_fusion.3
  1064.8 13.8 pad_add_fusion
  1094.4 12.0 fusion.79
  1172.7 31.8 %all-to-all-done.4 = bf16[4,2,196608]{2,1,0:T(2,128)(2,1)S(1)} async-done(((bf16[4,2,196608]{2,1,0:T(2,128)(2,1)}), bf16[4,2,196608]{2,1,0:T(2,128)(2,1)S(1)}, u32[]{:S(2)}, u32[]{:S(2)}) %all-to-all-start.4) | async-done | bytes 3145760 | tf_op jit(solution)/shard_map/all_to_all | solution.py:312
  1220.1 22.9 fusion.77
  1261.2 23.5 %multiply_reduce_fusion.11 = (f32[1536]{0:T(1024)S(1)}, f32[512]{0:T(512)S(1)}, f32[512,1536]{1,0:T(8,128)}) fusion(f32[512,1536]{1,0:T(8,128)S(1)} %copy-done.11, f32[512]{0:T(512)} %copy-done.73, f32[1536]{0:T(1024)S(1)} %copy-done.68, bf16[1536,6448]{1,0:T(8,128)(2,1)} %all-gather.10.cloned.1.call-done, bf16[512,48]{0,1:T(8,128)(2,1)} %copy-done.53, ...), kind=kOutput, calls=%fused_computation.96 | convolution fusion | flops 10172954624 | bytes 32718848 | tf_op jit(solution)/shard_map/tf,df->td/dot_general | solution.py:332
  1285.5 155.6 %reduce-scatter.8.cloned.1.call-done = f32[384,1536]{1,0:T(8,128)} async-done(((f32[3072,1536]{1,0:T(8,128)}), f32[384,1536]{1,0:T(8,128)}) %reduce-scatter.8.cloned.1.call-update) | async-done | bytes 2359312 | tf_op jit(solution)/shard_map/reduce_scatter | solution.py:364
  1441.1 643.4 %reduce-scatter.6.cloned.1.call-done = f32[192,6448]{1,0:T(8,128)} async-done(((f32[1536,6448]{1,0:T(8,128)}), f32[192,6448]{1,0:T(8,128)}) %reduce-scatter.6.cloned.1.call-update) | async-done | bytes 4952080 | tf_op jit(solution)/shard_map/reduce_scatter | solution.py:363
  2085.2 11.6 convolution_add_fusion
  2099.3 57.1 %all-reduce.10.cloned.1.call-done = f32[21392]{0:T(1024)} async-done(((f32[21392]{0:T(1024)}), f32[21392]{0:T(1024)}) %all-reduce.10.cloned.1.call-update) | async-done | bytes 85584
  2168.4 127.5 %all-reduce.12.cloned.1.call-done = (f32[192,6448]{1,0:T(8,128)}, f32[384,1536]{1,0:T(8,128)}) async-done(((f32[192,6448]{1,0:T(8,128)}, f32[384,1536]{1,0:T(8,128)}), (f32[192,6448]{1,0:T(8,128)}, f32[384,1536]{1,0:T(8,128)})) %all-reduce.12.cloned.1.call-update) | async-done | bytes 7311376 | tf_op jit(solution)/shard_map/psum | solution.py:367
  2295.9 13.9 multiply_subtract_fusion
  (426 shorter events, 406.3 us)
Async XLA Ops:
  7.2 75.4 %copy-start.10 = (f32[512,1536]{1,0:T(8,128)S(1)}, f32[512,1536]{1,0:T(8,128)}, u32[]{:S(2)}) copy-start(f32[512,1536]{1,0:T(8,128)} %param.15) | copy-start | bytes 9437188
  7.2 394.0 %all-gather.10.cloned.1.call-start = ((), (), s32[]{:S(2)}) async-start(), calls=%async_computation.9 | async-start | bytes 22560768 | tf_op jit(solution)/shard_map/all_gather | solution.py:122
  82.5 348.6 %copy-start.45 = (bf16[21392]{0:T(1024)(128)(2,1)}, bf16[21392]{0:T(1024)(128)(2,1)S(1)}, u32[]{:S(2)}) copy-start(bf16[21392]{0:T(1024)(128)(2,1)S(1)} %all-reduce.4) | copy-start | bytes 128356
  82.6 335.7 %copy-start.67 = (f32[1536]{0:T(1024)}, f32[1536]{0:T(1024)S(1)}, u32[]{:S(2)}) copy-start(f32[1536]{0:T(1024)S(1)} %slice.179) | copy-start | bytes 18436
  82.9 335.4 %copy-start.73 = (f32[512]{0:T(512)}, f32[512]{0:T(512)S(1)}, u32[]{:S(2)}) copy-start(f32[512]{0:T(512)S(1)} %add_rsqrt_fusion.1) | copy-start | bytes 6148
  419.8 7.4 all-to-all-start.1
  427.2 46.2 %all-to-all-start = ((bf16[512,4,768]{0,2,1:T(8,128)(2,1)}), bf16[512,4,768]{0,2,1:T(8,128)(2,1)S(1)}, u32[]{:S(2)}, u32[]{:S(2)}) async-start(bf16[512,4,768]{0,2,1:T(8,128)(2,1)} %bitcast.2), calls=%async_computation | async-start | bytes 6291456 | tf_op jit(solution)/shard_map/all_to_all | solution.py:138
  430.9 48.1 %all-gather.12.cloned.1.call-start = ((), (), s32[]{:S(2)}) async-start(), calls=%async_computation.10 | async-start | bytes 1310720 | tf_op jit(solution)/shard_map/all_gather | solution.py:142
  432.4 62.1 %copy-start.56 = (f32[1,1024]{1,0:T(1,128)}, f32[1,1024]{1,0:T(1,128)S(1)}, u32[]{:S(2)}) copy-start(f32[1,1024]{1,0:T(1,128)S(1)} %get-tuple-element.306) | copy-start | bytes 12292
  434.1 173.3 %all-gather.16.cloned.1.call-start = ((), (), s32[]{:S(2)}) async-start(), calls=%async_computation.15 | async-start | bytes 3538944 | tf_op jit(solution)/shard_map/all_gather | solution.py:36
  443.5 69.6 %copy-start.38 = (f32[8,256,12]{1,2,0:T(8,128)}, f32[8,256,12]{1,2,0:T(8,128)S(1)}, u32[]{:S(2)}) copy-start(f32[8,256,12]{1,2,0:T(8,128)S(1)} %get-tuple-element.297) | copy-start | bytes 294916
  482.3 7.7 collective-permute-start
  531.0 201.9 %all-gather.14.cloned.1.call-start = ((), (), s32[]{:S(2)}) async-start(), calls=%async_computation.11 | async-start | bytes 10616832 | tf_op jit(solution)/shard_map/all_gather | solution.py:123
  534.1 364.6 %copy-start.51 = (pred[256,256]{1,0:T(8,128)(4,1)}, pred[256,256]{1,0:T(8,128)(4,1)S(1)}, u32[]{:S(2)}) copy-start(pred[256,256]{1,0:T(8,128)(4,1)S(1)} %iota_compare_fusion) | copy-start | bytes 196612
  615.6 267.1 %copy-start.6 = (f32[12,64,128]{2,1,0:T(8,128)}, f32[12,64,128]{2,1,0:T(8,128)S(1)}, u32[]{:S(2)}) copy-start(f32[12,64,128]{2,1,0:T(8,128)S(1)} %broadcast_select_fusion.1) | copy-start | bytes 1179652
  654.5 41.7 %all-to-all-start.2 = ((bf16[4,2,196608]{2,1,0:T(2,128)(2,1)}), bf16[4,2,196608]{2,1,0:T(2,128)(2,1)}, u32[]{:S(2)}, u32[]{:S(2)}) async-start(bf16[4,2,196608]{2,1,0:T(2,128)(2,1)} %reshape.317), calls=%async_computation.2 | async-start | bytes 6291456 | tf_op jit(solution)/shard_map/all_to_all | solution.py:211
  659.9 86.3 %copy-start.40 = (f32[3072]{0:T(1024)}, f32[3072]{0:T(1024)S(1)}, u32[]{:S(2)}) copy-start(f32[3072]{0:T(1024)S(1)} %slice.202) | copy-start | bytes 36868
  753.7 76.0 %all-to-all-start.3 = ((f32[512,4,768]{0,2,1:T(8,128)}), f32[512,4,768]{0,2,1:T(8,128)}, u32[]{:S(2)}, u32[]{:S(2)}) async-start(f32[512,4,768]{0,2,1:T(8,128)} %bitcast.237), calls=%async_computation.3 | async-start | bytes 12582912 | tf_op jit(solution)/shard_map/all_to_all | solution.py:232
  758.9 207.4 %all-gather.18.cloned.1.call-start = ((), (), s32[]{:S(2)}) async-start(), calls=%async_computation.16 | async-start | bytes 3538944 | tf_op jit(solution)/shard_map/all_gather | solution.py:36
  864.6 354.4 %reduce-scatter.4.cloned.1.call-start = ((), (), s32[]{:S(2)}) async-start(), calls=%async_computation.12 | async-start | bytes 2621440 | tf_op jit(solution)/shard_map/reduce_scatter | solution.py:327
  939.9 70.6 %copy-start.8 = (f32[12,64,128,8]{2,3,1,0:T(8,128)}, f32[12,64,128,8]{2,3,1,0:T(8,128)S(1)}, u32[]{:S(2)}) copy-start(f32[12,64,128,8]{2,3,1,0:T(8,128)S(1)} %fusion.56) | copy-start | bytes 9437188
  1063.5 24.4 %collective-permute-start.1 = (f32[3,1024]{0,1:T(8,128)S(1)}, f32[3,1024]{0,1:T(8,128)S(1)}, u32[]{:S(2)}, u32[]{:S(2)}) collective-permute-start(f32[3,1024]{0,1:T(8,128)S(1)} %add_select_fusion), channel_id=1, source_target_pairs={{1,0},{2,1},{3,2},{4,3},{5,4},{6,5},{7,6},{9,8},{10,9},{11,10},{12... | collective-permute-start | bytes 36872 | tf_op jit(solution)/shard_map/ppermute | solution.py:31
  1093.3 347.8 %reduce-scatter.8.cloned.1.call-start = ((), (), s32[]{:S(2)}) async-start(), calls=%async_computation.14 | async-start | bytes 21233664 | tf_op jit(solution)/shard_map/reduce_scatter | solution.py:364
  1143.6 20.3 all-to-all-start.5
  1163.9 40.6 %all-to-all-start.4 = ((bf16[4,2,196608]{2,1,0:T(2,128)(2,1)}), bf16[4,2,196608]{2,1,0:T(2,128)(2,1)S(1)}, u32[]{:S(2)}, u32[]{:S(2)}) async-start(bf16[4,2,196608]{2,1,0:T(2,128)(2,1)} %reshape.321), calls=%async_computation.4 | async-start | bytes 6291456 | tf_op jit(solution)/shard_map/all_to_all | solution.py:312
  1167.6 916.8 %reduce-scatter.6.cloned.1.call-start = ((), (), s32[]{:S(2)}) async-start(), calls=%async_computation.13 | async-start | bytes 45121536 | tf_op jit(solution)/shard_map/reduce_scatter | solution.py:363
  1243.0 913.4 %all-reduce.10.cloned.1.call-start = ((), (), s32[]{:S(2)}) async-start(), calls=%async_computation.17 | async-start | bytes 172032
  1284.7 800.5 %copy-start.41 = (f32[3072]{0:T(1024)S(1)}, f32[3072]{0:T(1024)}, u32[]{:S(2)}) copy-start(f32[3072]{0:T(1024)} %copy-done.40) | copy-start | bytes 36868
  1285.4 1010.5 %all-reduce.12.cloned.1.call-start = ((), (), s32[]{:S(2)}) async-start(), calls=%async_computation.18 | async-start | bytes 14745600 | tf_op jit(solution)/shard_map/psum | solution.py:367
  2096.8 70.9 %copy-start.55 = (f32[2674]{0:T(1024)S(1)}, f32[2674]{0:T(1024)}, u32[]{:S(2)}) copy-start(f32[2674]{0:T(1024)} %param.23) | copy-start | bytes 32092
  2096.8 70.9 %copy-start.70 = (f32[2674]{0:T(1024)S(1)}, f32[2674]{0:T(1024)}, u32[]{:S(2)}) copy-start(f32[2674]{0:T(1024)} %param.25) | copy-start | bytes 32092
  2096.8 70.9 %copy-start.71 = (f32[2674]{0:T(1024)S(1)}, f32[2674]{0:T(1024)}, u32[]{:S(2)}) copy-start(f32[2674]{0:T(1024)} %param.24) | copy-start | bytes 32092
  (80 other events, 1143.3 us)
Sparse Core Ops, SparseCore 0:
  11.7 389.4 all-gather.9
  434.2 22.7 all-gather.11
  531.2 62.4 all-gather.15
  596.2 136.6 all-gather.13
  864.7 57.7 all-gather.17
  1093.4 30.0 reduce-scatter.3
  1127.8 313.2 reduce-scatter.7
  1445.5 638.8 reduce-scatter.5
  2088.4 67.9 all-reduce.9
  2158.8 137.0 all-reduce.11
where the time goes:
time: 2330 us; the launch traced here: 2320 us
  waiting for transfers between devices  1490 us (64%)
  matrix products  308 us (13%)
  local copies, waits for them, and re-layouts  181 us (8%)
  other arithmetic  181 us (8%)
  blocking collectives  118 us (5%)
  starting transfers between devices  28.5 us (1%)
    reduce_scatter x1, waiting for transfers between devices, per_device(): lax.psum_scatter(grad_in, 'shard', scatter_dimension=0, tiled=True)  643 us
    all_gather x1, waiting for transfers between devices, per_device(): lax.all_gather(weight_in.astype(jnp.bfloat16), 'shard', axis=0, tiled=True)  318 us
    reduce_scatter x1, waiting for transfers between devices, per_device(): lax.psum_scatter(grad_out, 'shard', scatter_dimension=0, tiled=True)  156 us
    psum x1, waiting for transfers between devices, per_device(): lax.psum((part_in, part_out, part_small), 'head')  128 us
    all_to_all x1, waiting for transfers between devices, per_device(): lax.all_to_all(d_y.reshape(tok_rows, head_count, head_width), 'head', spl...  70.6 us
    unnamed x1, blocking collectives  69.3 us
    unnamed x208, local copies, waits for them, and re-layouts  61.8 us
    unnamed x11, waiting for transfers between devices  57.3 us
  transfers between devices with their start and end apart: 18, of which 12 were waited for; matrix products, arithmetic and copies ran while one was open for 18% of the time, Pallas kernels for 0%

commit v1 on v0

v1 whole, which is shorter than its diff:
```python
import functools

import jax
import jax.numpy as jnp
from jax import lax
from jax.experimental import pallas as pl
from jax.experimental.pallas import tpu as pltpu
from jax.sharding import PartitionSpec as P

D = 1536
DI = 3072
HEADS = 48
HEADDIM = 64
NSTATE = 128
CONV = 4
BLOCK = 256
STEP = 5
XBC = 3328
HALO = 16
LANES = 128


EPSILON = 1e-05
BETA_FIRST = 0.9
BETA_SECOND = 0.95
ADAM_EPSILON = 1e-08
RATE_MATRIX = 0.02
RATE_SMALL = 0.2
DECAY_MATRIX = 0.1
F32 = jnp.float32
BF16 = jnp.bfloat16


def unpack(packed):
    offset = 0
    conv_weight = packed[offset : offset + CONV * XBC].reshape(CONV, XBC)
    offset = offset + CONV * XBC
    conv_bias = packed[offset : offset + XBC]
    offset = offset + XBC
    dt_bias = packed[offset : offset + HEADS]
    a_log = packed[offset + HEADS : offset + 2 * HEADS]
    skip_gain = packed[offset + 2 * HEADS : offset + 3 * HEADS]
    offset = offset + 3 * HEADS
    norm_gain = packed[offset : offset + DI]
    pre_gain = packed[offset + DI : offset + DI + D]
    return (conv_weight, conv_bias, dt_bias, a_log, skip_gain, norm_gain, pre_gain)


def adamw(weight, moment_one, moment_two, gradient, step_rate, weight_decay):
    moment_one = BETA_FIRST * moment_one + (1.0 - BETA_FIRST) * gradient
    moment_two = BETA_SECOND * moment_two + (1.0 - BETA_SECOND) * gradient * gradient
    first_hat = moment_one / (1.0 - BETA_FIRST**STEP)
    second_hat = moment_two / (1.0 - BETA_SECOND**STEP)
    weight = weight - step_rate * (
        first_hat / (jnp.sqrt(second_hat) + ADAM_EPSILON) + weight_decay * weight
    )
    return (moment_one, moment_two, weight)


def swap_core(value):
    peers = lax.axis_size("head")
    return lax.ppermute(value, "head", [(i, i ^ 1) for i in range(peers)])


def shift_chip(value, by):
    peers = lax.axis_size("head")
    chips = peers // 2
    return lax.ppermute(
        value, "head", [(i, ((i // 2 + by) % chips) * 2 + i % 2) for i in range(peers)]
    )


def gather_head(value):
    peers = lax.axis_size("head")
    chips = peers // 2
    mine = lax.axis_index("head")
    chip, core = mine // 2, mine % 2
    rows = value.shape[0]
    pieces = [(mine, value)]
    for by in range(1, chips):
        far = shift_chip(value, by)
        source = lax.rem(chip + chips - by, chips) * 2 + core
        pieces.append((source, far))
        pieces.append((lax.bitwise_xor(source, 1), swap_core(far)))
    pieces.append((lax.bitwise_xor(mine, 1), swap_core(value)))
    whole = jnp.zeros((peers * rows,) + value.shape[1:], value.dtype)
    for source, piece in pieces:
        whole = lax.dynamic_update_slice_in_dim(whole, piece, source * rows, 0)
    return whole


def sum_head(value):
    chips = lax.axis_size("head") // 2
    total = value
    for by in range(1, chips):
        total = total + shift_chip(value, by)
    return total + swap_core(total)


def shift_shard(value, by):
    peers = lax.axis_size("shard")
    pairs = [(i, i + by) for i in range(peers) if 0 <= i + by < peers]
    return lax.ppermute(value, "shard", pairs)


def split(value):
    high = value.astype(BF16)
    return high, (value - high.astype(F32)).astype(BF16)


def contract(a, b, dims):
    return lax.dot_general(a, b, (dims, ((), ())), preferred_element_type=F32)


NN = ((1,), (0,))
NT = ((1,), (1,))


def dot3(a, b, dims):
    (ah, al), (bh, bl) = a, b
    return contract(ah, bh, dims) + (contract(ah, bl, dims) + contract(al, bh, dims))


def running(value, forward):
    rows = value.shape[0]
    here = lax.broadcasted_iota(jnp.int32, (rows, rows), 0)
    other = lax.broadcasted_iota(jnp.int32, (rows, rows), 1)
    mask = jnp.where(here >= other if forward else here <= other, 1.0, 0.0).astype(BF16)
    high, mid = split(value)
    low = ((value - high.astype(F32)) - mid.astype(F32)).astype(BF16)
    return contract(mask, high, NN) + (contract(mask, mid, NN) + contract(mask, low, NN))


def spread_heads(value, base, width):
    rows = value.shape[0]
    left = lax.broadcasted_iota(jnp.int32, (rows, LANES), 1) < HEADDIM
    tiles = []
    for pair in range(width // LANES):
        lane = base + 2 * pair
        tiles.append(
            jnp.where(
                left,
                jnp.broadcast_to(value[:, lane : lane + 1], (rows, LANES)),
                jnp.broadcast_to(value[:, lane + 1 : lane + 2], (rows, LANES)),
            )
        )
    return jnp.concatenate(tiles, axis=1)


def gather_heads(value, base):
    width = value.shape[1]
    channel = lax.broadcasted_iota(jnp.int32, (width, LANES), 0)
    lane = lax.broadcasted_iota(jnp.int32, (width, LANES), 1)
    chosen = (channel >= (lane - base) * HEADDIM) & (channel < (lane - base + 1) * HEADDIM)
    mask = jnp.where(chosen, 1.0, 0.0).astype(BF16)
    high, low = split(value)
    return contract(high, mask, NN) + contract(low, mask, NN)


def half_masks(rows):
    lane = lax.broadcasted_iota(jnp.int32, (rows, LANES), 1)
    return lane < HEADDIM, lane >= HEADDIM


def pair_product(mats, value):
    high, low = split(value)
    zero = jnp.zeros_like(high)
    parts = []
    for mat, keep in zip(mats, half_masks(value.shape[0])):
        mh, ml = split(mat)
        vh = jnp.where(keep, high, zero)
        both = jnp.concatenate([vh, jnp.where(keep, low, zero)], axis=1)
        wide = contract(mh, both, NN)
        parts.append(wide[:, :LANES] + (wide[:, LANES:] + contract(ml, vh, NN)))
    return parts[0] + parts[1]


def prepare_kernel(
    base, x_ref, b_ref, c_ref, misc_ref, hx_ref, hb_ref, hc_ref, taps_ref, heads_ref,
    act_ref, der_ref, time_ref, state_ref, decay_ref, rows_ref, total_ref,
):
    step = pl.program_id(0)
    width = x_ref.shape[1]

    @pl.when(step == 0)
    def _():
        rows_ref[0:8, 0:width] = hx_ref[...].astype(F32)[8:16]
        rows_ref[0:8, width : width + NSTATE] = hb_ref[...].astype(F32)[8:16]
        rows_ref[0:8, width + NSTATE :] = hc_ref[...].astype(F32)[8:16]
        state_ref[...] = jnp.zeros_like(state_ref)
        total_ref[...] = jnp.zeros_like(total_ref)

    rows_ref[8:, 0:width] = x_ref[...].astype(F32)
    rows_ref[8:, width : width + NSTATE] = b_ref[...].astype(F32)
    rows_ref[8:, width + NSTATE :] = c_ref[...].astype(F32)
    for start in range(0, width + 2 * NSTATE, LANES):
        cols = slice(start, start + LANES)
        conv = taps_ref[CONV : CONV + 1, cols]
        for tap in range(CONV):
            first = 8 - (CONV - 1) + tap
            conv = conv + taps_ref[tap : tap + 1, cols] * rows_ref[first : first + BLOCK, cols]
        sig = jax.nn.sigmoid(conv)
        act_ref[:, cols] = conv * sig
        der_ref[:, cols] = sig * (1.0 + conv * (1.0 - sig))
    rows_ref[0:8, :] = rows_ref[BLOCK : BLOCK + 8, :]

    size = jax.nn.softplus(misc_ref[...].astype(F32) + heads_ref[0:1, :])
    log_decay = running(size * heads_ref[1:2, :], True)
    time_ref[:, :LANES] = size
    time_ref[:, LANES:] = log_decay
    last = log_decay[BLOCK - 1 : BLOCK, :]
    weighted = act_ref[:, 0:width] * spread_heads(jnp.exp(last - log_decay) * size, base, width)
    b_turned = jnp.transpose(act_ref[:, width : width + NSTATE])
    state_ref[...] = state_ref[...] * spread_heads(jnp.exp(last), base, width) + dot3(
        split(b_turned), split(weighted), NN
    )
    total_ref[...] = total_ref[...] + jnp.broadcast_to(last, total_ref.shape)
    decay_ref[...] = spread_heads(jnp.exp(total_ref[...]), base, width)


def forward_kernel(
    base, act_ref, time_ref, gate_ref, dmix_ref, chan_ref, prior_ref,
    ymix_ref, yssm_ref, sums_ref, before_ref, final_ref,
):
    step = pl.program_id(0)
    width = gate_ref.shape[1]

    @pl.when(step == 0)
    def _():
        final_ref[...] = prior_ref[...]

    state = final_ref[...]
    before_ref[...] = state
    size, log_decay = time_ref[:, :LANES], time_ref[:, LANES:]
    decay_rows = jnp.transpose(log_decay)
    last = log_decay[BLOCK - 1 : BLOCK, :]
    b_act, c_act = act_ref[:, width : width + NSTATE], act_ref[:, width + NSTATE :]
    c_parts = split(c_act)
    here = lax.broadcasted_iota(jnp.int32, (BLOCK, BLOCK), 0)
    other = lax.broadcasted_iota(jnp.int32, (BLOCK, BLOCK), 1)
    causal = here >= other
    scores = dot3(c_parts, split(b_act), NT)
    reach = jnp.exp(log_decay)
    carried = dot3(c_parts, split(state), NN)
    square = jnp.zeros((BLOCK, 1), F32)
    cross = jnp.zeros((BLOCK, 1), F32)
    for pair in range(width // LANES):
        cols = slice(pair * LANES, (pair + 1) * LANES)
        lane = base + 2 * pair
        x_pair = act_ref[:, cols]
        scaled = x_pair * spread_heads(size[:, lane : lane + 2], 0, LANES)
        mats = []
        for q in range(2):
            gap = log_decay[:, lane + q : lane + q + 1] - decay_rows[lane + q : lane + q + 1, :]
            mats.append(jnp.exp(jnp.where(causal, gap, -jnp.inf)) * scores)
        y_ssm = pair_product(mats, scaled) + carried[:, cols] * spread_heads(
            reach[:, lane : lane + 2], 0, LANES
        )
        yssm_ref[:, cols] = y_ssm
        y_mix = (y_ssm + chan_ref[0:1, cols] * x_pair).astype(BF16)
        ymix_ref[:, cols] = y_mix
        gate = gate_ref[:, cols].astype(F32)
        gated = y_mix.astype(F32) * (gate * jax.nn.sigmoid(gate))
        square = square + jnp.sum(gated * gated, axis=1, keepdims=True)
        cross = cross + jnp.sum(
            dmix_ref[:, cols] * chan_ref[1:2, cols] * gated, axis=1, keepdims=True
        )
    lane_id = lax.broadcasted_iota(jnp.int32, (BLOCK, LANES), 1)
    both = jnp.where(lane_id == 0, square, jnp.where(lane_id == 1, cross, 0.0))
    sums_ref[...] = jnp.transpose(both)[0:8, :]
    weighted = act_ref[:, 0:width] * spread_heads(jnp.exp(last - log_decay) * size, base, width)
    final_ref[...] = state * spread_heads(jnp.exp(last), base, width) + dot3(
        split(jnp.transpose(b_act)), split(weighted), NN
    )


def gate_kernel(
    base, c_ref, time_ref, gate_ref, dmix_ref, ymix_ref, sums_ref, chan_ref,
    mixed_ref, dgate_ref, dy_ref, state_ref, gain_ref,
):
    step = pl.program_id(0)
    width = gate_ref.shape[1]

    @pl.when(step == 0)
    def _():
        state_ref[...] = jnp.zeros_like(state_ref)
        gain_ref[...] = jnp.zeros_like(gain_ref)

    sums = jnp.transpose(jnp.concatenate([sums_ref[...]] * (LANES // 8), axis=0))
    scale = lax.rsqrt(sums[:, 0:1] / DI + EPSILON)
    unit_mean = scale * (sums[:, 1:2] / DI)
    log_decay = time_ref[...]
    last = log_decay[BLOCK - 1 : BLOCK, :]
    reach = jnp.exp(log_decay)
    c_turned = split(jnp.transpose(c_ref[...]))
    for pair in range(width // LANES):
        cols = slice(pair * LANES, (pair + 1) * LANES)
        lane = base + 2 * pair
        gate = gate_ref[:, cols].astype(F32)
        sig = jax.nn.sigmoid(gate)
        silu = gate * sig
        y_mix = ymix_ref[:, cols].astype(F32)
        d_mixed = dmix_ref[:, cols]
        gain = chan_ref[1:2, cols]
        unit = y_mix * silu * scale
        mixed_ref[:, cols] = (unit * gain).astype(BF16)
        gain_ref[:, cols] = gain_ref[:, cols] + jnp.sum(d_mixed * unit, axis=0, keepdims=True)
        d_gated = scale * (d_mixed * gain - unit * unit_mean)
        d_y = d_gated * silu
        dy_ref[:, cols] = d_y
        dgate_ref[:, cols] = (d_gated * y_mix * sig * (1.0 + gate * (1.0 - sig))).astype(BF16)
        scaled = d_y * spread_heads(reach[:, lane : lane + 2], 0, LANES)
        state_ref[:, cols] = state_ref[:, cols] * spread_heads(
            jnp.exp(last[:, lane : lane + 2]), 0, LANES
        ) + dot3(c_turned, split(scaled), NN)


def backward_kernel(
    base, local_heads, act_ref, der_ref, time_ref, dy_ref, yssm_ref, before_ref, final_ref, after_ref,
    misc_ref, x_ref, b_ref, c_ref, px_ref, pb_ref, pc_ref, hx_ref, hb_ref, hc_ref,
    taps_ref, heads_ref, chan_ref,
    drest_ref, dbc_ref, first_ref, rest_ref, gtap_ref, gskip_ref, ghead_ref,
    state_ref, tail_ref, next_ref, rows_ref, dact_ref,
):
    step = pl.program_id(0)
    steps = pl.num_programs(0)
    width = dy_ref.shape[1]

    @pl.when(step == 0)
    def _():
        state_ref[...] = after_ref[...]
        product = after_ref[...] * final_ref[...]
        tail = jnp.sum(gather_heads(product, base), axis=0, keepdims=True)
        tail_ref[...] = jnp.broadcast_to(tail, tail_ref.shape)
        next_ref[BLOCK:, :] = jnp.zeros((8, width + 2 * NSTATE), F32)
        gtap_ref[...] = jnp.zeros_like(gtap_ref)
        gskip_ref[...] = jnp.zeros_like(gskip_ref)
        ghead_ref[...] = jnp.zeros_like(ghead_ref)

    state = state_ref[...]
    size, log_decay = time_ref[:, :LANES], time_ref[:, LANES:]
    decay_rows = jnp.transpose(log_decay)
    last = log_decay[BLOCK - 1 : BLOCK, :]
    b_act, c_act = act_ref[:, width : width + NSTATE], act_ref[:, width + NSTATE :]
    b_parts, c_parts = split(b_act), split(c_act)
    here = lax.broadcasted_iota(jnp.int32, (BLOCK, BLOCK), 0)
    other = lax.broadcasted_iota(jnp.int32, (BLOCK, BLOCK), 1)
    causal = other >= here
    scores = dot3(b_parts, c_parts, NT)
    reach = jnp.exp(log_decay)
    to_end = jnp.exp(last - log_decay)
    state_parts = split(state)
    carried = dot3(b_parts, state_parts, NN)
    masks = half_masks(BLOCK)
    pairs = jnp.zeros((BLOCK, BLOCK), F32)
    along = jnp.zeros((BLOCK, LANES), F32)
    for pair in range(width // LANES):
        cols = slice(pair * LANES, (pair + 1) * LANES)
        lane = base + 2 * pair
        x_pair, dy_pair = act_ref[:, cols], dy_ref[:, cols]
        size_pair = spread_heads(size[:, lane : lane + 2], 0, LANES)
        xs_high, xs_low = split(x_pair * size_pair)
        dy_high, dy_low = split(dy_pair)
        zero = jnp.zeros_like(xs_high)
        mats = []
        for q in range(2):
            gap = decay_rows[lane + q : lane + q + 1, :] - log_decay[:, lane + q : lane + q + 1]
            weight = jnp.exp(jnp.where(causal, gap, -jnp.inf))
            mats.append(weight * scores)
            xh = jnp.where(masks[q], xs_high, zero)
            xl = jnp.where(masks[q], xs_low, zero)
            found = contract(
                jnp.concatenate([xh, xl], axis=1), jnp.concatenate([dy_high, dy_high], axis=1), NT
            ) + contract(xh, dy_low, NT)
            pairs = pairs + found * weight
        q_all = pair_product(mats, dy_pair) + carried[:, cols] * spread_heads(
            to_end[:, lane : lane + 2], 0, LANES
        )
        dx = q_all * size_pair + chan_ref[0:1, cols] * dy_pair
        next_ref[0:BLOCK, cols] = dx * der_ref[:, cols]
        gskip_ref[:, cols] = gskip_ref[:, cols] + jnp.sum(dy_pair * x_pair, axis=0, keepdims=True)
        dact_ref[:, cols] = x_pair * q_all
    pairs_parts = split(pairs)
    turned_parts = split(jnp.transpose(pairs))
    weighted = act_ref[:, 0:width] * spread_heads(to_end * size, base, width)
    d_b = dot3(pairs_parts, c_parts, NN) + dot3(split(weighted), state_parts, NT)
    scaled = split(dy_ref[...] * spread_heads(reach, base, width))
    d_c = dot3(turned_parts, b_parts, NN) + dot3(scaled, split(before_ref[...]), NT)
    next_ref[0:BLOCK, width : width + NSTATE] = d_b * der_ref[:, width : width + NSTATE]
    next_ref[0:BLOCK, width + NSTATE :] = d_c * der_ref[:, width + NSTATE :]
    state_ref[...] = state * spread_heads(jnp.exp(last), base, width) + dot3(
        split(jnp.transpose(c_act)), scaled, NN
    )

    along = gather_heads(dy_ref[...] * yssm_ref[...], base)
    across = gather_heads(dact_ref[...], base)
    d_log = running(along - size * across, False) + tail_ref[0:1, :]
    tail_ref[...] = jnp.broadcast_to(d_log[0:1, :], tail_ref.shape)
    lane_id = lax.broadcasted_iota(jnp.int32, (BLOCK, LANES), 1)
    mine = (lane_id >= base) & (lane_id < base + local_heads)
    d_size = across + d_log * heads_ref[1:2, :]
    d_dt = jnp.where(
        mine, d_size * jax.nn.sigmoid(misc_ref[...].astype(F32) + heads_ref[0:1, :]), 0.0
    )
    drest_ref[:, width:] = d_dt.astype(BF16)
    ghead_ref[0:1, :] = ghead_ref[0:1, :] + jnp.sum(d_dt, axis=0, keepdims=True)
    ghead_ref[1:2, :] = ghead_ref[1:2, :] + jnp.sum(d_log * size, axis=0, keepdims=True)

    begin = step == steps - 1
    for kept, first, start in (
        (px_ref, hx_ref, slice(0, width)),
        (pb_ref, hb_ref, slice(width, width + NSTATE)),
        (pc_ref, hc_ref, slice(width + NSTATE, width + 2 * NSTATE)),
    ):
        rows_ref[0:8, start] = jnp.where(begin, first[...].astype(F32)[8:16], kept[...].astype(F32)[8:16])
    rows_ref[8:, 0:width] = x_ref[...].astype(F32)
    rows_ref[8:, width : width + NSTATE] = b_ref[...].astype(F32)
    rows_ref[8:, width + NSTATE :] = c_ref[...].astype(F32)
    for start in range(0, width + 2 * NSTATE, LANES):
        cols = slice(start, start + LANES)
        d_conv = next_ref[0:BLOCK, cols]
        d_raw = jnp.zeros((BLOCK, LANES), F32)
        for tap in range(CONV):
            ahead = CONV - 1 - tap
            d_raw = d_raw + taps_ref[tap : tap + 1, cols] * next_ref[ahead : ahead + BLOCK, cols]
            first = 8 - (CONV - 1) + tap
            gtap_ref[tap : tap + 1, cols] = gtap_ref[tap : tap + 1, cols] + jnp.sum(
                d_conv * rows_ref[first : first + BLOCK, cols], axis=0, keepdims=True
            )
        gtap_ref[CONV : CONV + 1, cols] = gtap_ref[CONV : CONV + 1, cols] + jnp.sum(
            d_conv, axis=0, keepdims=True
        )
        if start < width:
            drest_ref[:, cols] = d_raw.astype(BF16)
        else:
            dbc_ref[start - width : start - width + LANES, :] = jnp.transpose(d_raw)

        @pl.when(step == 0)
        def _():
            rest_ref[:, cols] = d_raw[BLOCK - 16 :]

    next_ref[BLOCK:, :] = next_ref[0:8, :]
    first_ref[...] = next_ref[0:8, :]


def chain_kernel(direction, own_ref, decay_ref, prior_ref, inbox, outbox, send_sems, recv_sems):
    peers = lax.axis_size("shard")
    mine = lax.axis_index("shard")
    has_source = mine > 0 if direction > 0 else mine < peers - 1
    has_target = mine < peers - 1 if direction > 0 else mine > 0
    source, target = mine - direction, mine + direction
    barrier = pltpu.get_barrier_semaphore()

    @pl.when(has_source)
    def _():
        pl.semaphore_signal(
            barrier, inc=1, device_id={"shard": source}, device_id_type=pl.DeviceIdType.MESH
        )

    @pl.when(has_target)
    def _():
        pl.semaphore_wait(barrier, 1)

    count = send_sems.shape[0]
    rows = inbox.shape[0] // count

    def copy(piece):
        at = pl.ds(piece * rows, rows)
        return pltpu.make_async_remote_copy(
            src_ref=outbox.at[at],
            dst_ref=inbox.at[at],
            send_sem=send_sems.at[piece],
            recv_sem=recv_sems.at[piece],
            device_id={"shard": target},
            device_id_type=pl.DeviceIdType.MESH,
        )

    for piece in range(count):
        at = slice(piece * rows, (piece + 1) * rows)

        @pl.when(has_source)
        def _():
            copy(piece).wait_recv()
            prior_ref[at, :] = inbox[at, :]

        @pl.when(jnp.logical_not(has_source))
        def _():
            prior_ref[at, :] = jnp.zeros((rows, inbox.shape[1]), F32)

        @pl.when(has_target)
        def _():
            outbox[at, :] = prior_ref[at, :] * decay_ref[0:1, :] + own_ref[at, :]
            copy(piece).start()

    @pl.when(has_target)
    def _():
        for piece in range(count):
            copy(piece).wait_send()


PIECES = 8
VMEM_LIMIT = 48 * 1024 * 1024


def chain(own, decay, direction):
    shape = own.shape
    return pl.pallas_call(
        functools.partial(chain_kernel, direction),
        out_shape=jax.ShapeDtypeStruct(shape, F32),
        in_specs=[pl.BlockSpec(memory_space=pltpu.VMEM)] * 2,
        out_specs=pl.BlockSpec(memory_space=pltpu.VMEM),
        scratch_shapes=[
            pltpu.VMEM(shape, F32),
            pltpu.VMEM(shape, F32),
            pltpu.SemaphoreType.DMA((PIECES,)),
            pltpu.SemaphoreType.DMA((PIECES,)),
        ],
        compiler_params=pltpu.CompilerParams(
            collective_id=1,
            has_side_effects=True,
            vmem_limit_bytes=VMEM_LIMIT,
        ),
        name="carry_forward",
    )(own, decay)


def blocked(kernel, name, steps, operands, results, scratch, flops, moved):
    return pl.pallas_call(
        kernel,
        grid=(steps,),
        in_specs=[pl.BlockSpec(block, index) for _, block, index in operands],
        out_specs=[pl.BlockSpec(block, index) for _, _, block, index in results],
        out_shape=[jax.ShapeDtypeStruct(shape, kind) for shape, kind, _, _ in results],
        scratch_shapes=scratch,
        compiler_params=pltpu.CompilerParams(
            dimension_semantics=("arbitrary",), vmem_limit_bytes=VMEM_LIMIT
        ),
        cost_estimate=pl.CostEstimate(flops=flops, bytes_accessed=moved, transcendentals=0),
        name=name,
    )(*[array for array, _, _ in operands])


RING_ROWS = 4
MESH = pl.DeviceIdType.MESH


def ring_position(shard, peers):
    across = peers // RING_ROWS
    row, col = lax.div(shard, across), lax.rem(shard, across)
    turn = RING_ROWS - 1 - row
    inner = jnp.where(lax.rem(turn, 2) == 0, col - 1, across - 1 - col)
    return jnp.where(col == 0, row, RING_ROWS + turn * (across - 1) + inner)


def ring_shard(position, peers):
    across = peers // RING_ROWS
    place = lax.rem(position + 2 * peers, peers)
    after = jnp.maximum(place - RING_ROWS, 0)
    turn, inner = lax.div(after, across - 1), lax.rem(after, across - 1)
    col = jnp.where(lax.rem(turn, 2) == 0, inner + 1, across - 1 - inner)
    back = (RING_ROWS - 1 - turn) * across + col
    return jnp.where(place < RING_ROWS, jnp.minimum(place, RING_ROWS - 1) * across, back)


def cut_rows(rows, tile):
    parts = 2 if rows % (4 * tile) == 0 else 1
    half = -(-rows // (2 * tile)) * tile
    pieces = []
    for start, length, way in ((0, half, 1), (half, rows - half, -1)):
        size = length // parts
        pieces += [(start + i * size, size, way) for i in range(parts)]
    return sorted(pieces, key=lambda piece: (piece[0] - (half if piece[2] < 0 else 0), -piece[2]))


def greet(others):
    barrier = pltpu.get_barrier_semaphore()
    for device in others:
        pl.semaphore_signal(barrier, inc=1, device_id=device, device_id_type=MESH)
    return barrier


def remote(source, target, send, recv, device):
    return pltpu.make_async_remote_copy(
        src_ref=source, dst_ref=target, send_sem=send, recv_sem=recv, device_id=device, device_id_type=MESH
    )


def head_peers():
    peers = lax.axis_size("head")
    mine = lax.axis_index("head")
    chips = peers // 2
    chip, core = lax.div(mine, 2), lax.rem(mine, 2)
    there = [lax.rem(chip + by, chips) * 2 + core for by in range(1, chips)]
    source = [lax.rem(chip + chips - by, chips) * 2 + core for by in range(1, chips)]
    return mine + 1 - 2 * core, there, source


def worker_of(head, shard, heads, peers):
    stored, worked = shard * heads + head, head * peers + shard
    target = (lax.div(stored, peers), lax.rem(stored, peers))
    origin = (lax.rem(worked, heads), lax.div(worked, heads))
    return target, origin, stored == worked


def home_of(head, shard, heads, peers):
    target, origin, at_home = worker_of(head, shard, heads, peers)
    return origin, target, at_home


def greet_across(barrier, origin, at_home, usual):
    @pl.when(jnp.logical_not(at_home))
    def _():
        pl.semaphore_signal(barrier, inc=1, device_id=origin, device_id_type=MESH)
        pl.semaphore_wait(barrier, usual + 1)

    @pl.when(at_home)
    def _():
        pl.semaphore_wait(barrier, usual)


class HeadGather:
    def __init__(self, own, whole, sems):
        peers = lax.axis_size("head")
        mine = lax.axis_index("head")
        self.sibling, self.there, self.source = head_peers()
        rows = whole.shape[0] // peers
        hint = 16 if whole.dtype == BF16 else 8
        self.at = lambda owner: whole.at[pl.ds(pl.multiple_of(owner * rows, hint), rows)]
        self.own, self.mine = own, mine
        self.far_send, self.far_recv, self.near_send, self.near_recv = sems

    def far(self, by):
        return remote(
            self.own, self.at(self.mine), self.far_send.at[by], self.far_recv.at[by], {"head": self.there[by]}
        )

    def near(self, by):
        source = self.own if by < 0 else self.at(self.source[by])
        target = self.at(self.mine) if by < 0 else self.at(self.source[by])
        return remote(
            source, target, self.near_send.at[by + 1], self.near_recv.at[by + 1], {"head": self.sibling}
        )

    def start(self):
        for by in range(len(self.there)):
            self.far(by).start()
        self.near(-1).start()

    def pass_on(self):
        for by in range(len(self.there)):
            self.far(by).wait_recv()
            self.near(by).start()

    def finish(self):
        for by in range(-1, len(self.there)):
            self.near(by).wait_recv()

    def drain(self):
        for by in range(len(self.there)):
            self.far(by).wait_send()
        for by in range(-1, len(self.there)):
            self.near(by).wait_send()


def gather_kernel(ring_out, pieces, out_pieces, small_ref, chunk_ref, input_ref, cot_ref, out_ref, *refs):
    full_ref, normed_ref, cot_full_ref, projected_ref, smalls_ref, before_ref = refs[:6]
    refs = refs[6:]
    if ring_out:
        full_out_ref, refs = refs[0], refs[1:]
    (
        full, normed, cot_own, projected, inbox, rim, small_send, small_recv, ring_send, ring_recv,
        far_send, far_recv, near_send, near_recv, cot_far_send, cot_far_recv, cot_near_send, cot_near_recv,
        rim_send, rim_recv, local_sems, tile_sems,
    ) = refs[:22]
    if ring_out:
        full_out, piece_send, piece_recv, out_send, out_recv = refs[22:]
    peers, heads = lax.axis_size("shard"), lax.axis_size("head")
    shard, head = lax.axis_index("shard"), lax.axis_index("head")
    sibling, there, _ = head_peers()
    rows, tokens = chunk_ref.shape[0], input_ref.shape[0]
    others = [lax.rem(shard + by, peers) for by in range(1, peers)]
    barrier = greet(
        [{"shard": other} for other in others]
        + [{"head": other} for other in there]
        + [{"head": sibling}]
    )
    usual = peers - 1 + len(there) + 1
    if ring_out:
        target, origin, at_home = worker_of(head, shard, heads, peers)
        greet_across(barrier, origin, at_home, usual)
    else:
        pl.semaphore_wait(barrier, usual)
    place = ring_position(shard, peers)
    following, preceding = ring_shard(place + 1, peers), ring_shard(place - 1, peers)
    small_copies = [
        remote(
            small_ref, inbox.at[by], small_send.at[by], small_recv.at[by], {"shard": others[by]}
        )
        for by in range(peers - 1)
    ]
    for copy in small_copies:
        copy.start()

    def hop(chunk, whole, cuts, sends, recvs, index, step):
        first, size, way = cuts[index]
        owner = ring_shard(place - way * step, peers)
        each = whole.shape[0] // peers
        at = whole.at[pl.ds(pl.multiple_of(owner * each + first, 16), size)]
        return remote(
            chunk.at[pl.ds(first, size)] if step == 0 and chunk is not None else at,
            at,
            sends.at[index, step],
            recvs.at[index, step],
            {"shard": following if way > 0 else preceding},
        )

    in_hop = functools.partial(hop, chunk_ref, full, pieces, ring_send, ring_recv)
    for index in range(len(pieces)):
        in_hop(index, 0).start()
    keep = pltpu.make_async_copy(
        chunk_ref, full.at[pl.ds(pl.multiple_of(shard * rows, 16), rows)], local_sems.at[0]
    )
    keep.start()

    for copy in small_copies:
        copy.wait_recv()
    smalls_ref[pl.ds(shard, 1)] = small_ref[...][None]
    gain = small_ref[SMALL_ROWS:, :].astype(F32)
    for by in range(1, peers):
        from_there = lax.rem(shard + peers - by, peers)
        smalls_ref[pl.ds(from_there, 1)] = inbox[by - 1][None]
        gain = gain + inbox[by - 1, SMALL_ROWS:, :].astype(F32)
    gain = jnp.concatenate([gain[i : i + 1, :] for i in range(D // LANES)], axis=1)
    tile = 128
    for start in range(0, tokens, tile):
        value = input_ref[pl.ds(start, tile), :]
        scale = lax.rsqrt(jnp.mean(value * value, axis=-1, keepdims=True) + EPSILON)
        at = pl.ds(pl.multiple_of(head * tokens + start, tile), tile)
        normed[at, :] = (value * scale * gain).astype(BF16)
    mine = pl.ds(pl.multiple_of(head * tokens, 16), tokens)
    normed_gather = HeadGather(normed.at[mine], normed, (far_send, far_recv, near_send, near_recv))
    normed_gather.start()
    for start in range(0, tokens, tile):
        at = pl.ds(start, tile)
        cot_own[at, :] = cot_ref[at, :].astype(BF16)
    cot_gather = HeadGather(
        cot_own, cot_full_ref, (cot_far_send, cot_far_recv, cot_near_send, cot_near_recv)
    )
    cot_stay = pltpu.make_async_copy(cot_own, cot_full_ref.at[mine], local_sems.at[1])
    cot_stay.start()

    if ring_out:
        each = out_ref.shape[0]
        piece_copy = remote(
            out_ref, full_out.at[pl.ds(pl.multiple_of(target[1] * each, 16), each)],
            piece_send, piece_recv, target,
        )

        @pl.when(at_home)
        def _():
            full_out[pl.ds(pl.multiple_of(shard * each, 16), each), :] = out_ref[...]

        @pl.when(jnp.logical_not(at_home))
        def _():
            piece_copy.start()

    for step in range(1, peers - 1):
        for index in range(len(pieces)):
            in_hop(index, step - 1).wait_recv()
            in_hop(index, step).start()
        if step == min(5, peers - 2):
            normed_gather.pass_on()
            cot_gather.start()
    for index in range(len(pieces)):
        in_hop(index, peers - 2).wait_recv()
    keep.wait()
    normed_gather.finish()
    rim_copy = remote(
        normed.at[pl.ds(heads * tokens - HALO, HALO)], rim, rim_send, rim_recv,
        {"shard": lax.rem(shard + 1, peers)},
    )
    rim_copy.start()
    out_copies = [
        pltpu.make_async_copy(full, full_ref, local_sems.at[2]),
        pltpu.make_async_copy(normed, normed_ref, local_sems.at[3]),
    ]
    for copy in out_copies:
        copy.start()

    tiles = heads * tokens // BLOCK

    def tile_copy(number):
        at = pl.ds(pl.multiple_of(number * BLOCK, BLOCK), BLOCK)
        return pltpu.make_async_copy(projected.at[at], projected_ref.at[at], tile_sems.at[number])

    def project(number, carry):
        at = pl.ds(pl.multiple_of(number * BLOCK, BLOCK), BLOCK)
        projected[at, :] = contract(normed[at, :], full[...], NN).astype(BF16)
        tile_copy(number).start()
        return carry

    if ring_out:

        @pl.when(jnp.logical_not(at_home))
        def _():
            piece_copy.wait()

        out_hop = functools.partial(hop, None, full_out, out_pieces, out_send, out_recv)
        for step in range(peers - 1):
            for index in range(len(out_pieces)):
                if step:
                    out_hop(index, step - 1).wait_recv()
                out_hop(index, step).start()
            low, high = min(step, tiles), min(step + 1, tiles) if step < peers - 2 else tiles
            if low < high:
                lax.fori_loop(low, high, project, 0)
        for index in range(len(out_pieces)):
            out_hop(index, peers - 2).wait_recv()
        out_copies.append(pltpu.make_async_copy(full_out, full_out_ref, local_sems.at[4]))
        out_copies[-1].start()
    else:
        lax.fori_loop(0, tiles, project, 0)
    cot_gather.pass_on()
    rim_copy.wait_recv()
    before = contract(rim[...], full[...], NN)
    before_ref[...] = jnp.where(shard > 0, before, 0.0).astype(BF16)

    cot_gather.finish()
    cot_gather.drain()
    normed_gather.drain()
    for copy in small_copies:
        copy.wait_send()
    for index in range(len(pieces)):
        for step in range(peers - 1):
            in_hop(index, step).wait_send()
    rim_copy.wait_send()
    cot_stay.wait()
    for number in range(tiles):
        tile_copy(number).wait()
    for copy in out_copies:
        copy.wait()
    if ring_out:
        for index in range(len(out_pieces)):
            for step in range(peers - 1):
                out_hop(index, step).wait_send()


SMALL_ROWS = 32


def gather_start(small, chunk, layer_input, cotangent, out_rows):
    peers, heads = lax.axis_size("shard"), lax.axis_size("head")
    tokens = layer_input.shape[0]
    chips = heads // 2
    piece_rows = out_rows.shape[0]
    ring_out = piece_rows % 32 == 0
    pieces = cut_rows(chunk.shape[0], 16)
    out_pieces = cut_rows(piece_rows, 16) if ring_out else []
    inside = pl.BlockSpec(memory_space=pltpu.VMEM)
    outside = pl.BlockSpec(memory_space=pl.ANY)
    sems = pltpu.SemaphoreType.DMA
    group, cols = heads * tokens, chunk.shape[1]
    full_out_shape = (peers * piece_rows, D)
    head_sems = [sems((chips - 1,)), sems((chips - 1,)), sems((chips,)), sems((chips,))]
    return pl.pallas_call(
        functools.partial(gather_kernel, ring_out, pieces, out_pieces),
        out_shape=[
            jax.ShapeDtypeStruct((D, cols), BF16),
            jax.ShapeDtypeStruct((group, D), BF16),
            jax.ShapeDtypeStruct((group, D), BF16),
            jax.ShapeDtypeStruct((group, cols), BF16),
            jax.ShapeDtypeStruct((peers,) + small.shape, BF16),
            jax.ShapeDtypeStruct((HALO, cols), BF16),
        ]
        + ([jax.ShapeDtypeStruct(full_out_shape, BF16)] if ring_out else []),
        in_specs=[inside] * 4 + [inside if ring_out else outside],
        out_specs=[outside] * 4 + [inside] * 2 + ([outside] if ring_out else []),
        scratch_shapes=[
            pltpu.VMEM((D, cols), BF16),
            pltpu.VMEM((group, D), BF16),
            pltpu.VMEM((tokens, D), BF16),
            pltpu.VMEM((group, cols), BF16),
            pltpu.VMEM((peers - 1,) + small.shape, BF16),
            pltpu.VMEM((HALO, D), BF16),
            sems((peers - 1,)),
            sems((peers - 1,)),
            sems((len(pieces), peers - 1)),
            sems((len(pieces), peers - 1)),
            *head_sems,
            *head_sems,
            sems(()),
            sems(()),
            sems((5,)),
            sems((group // BLOCK,)),
        ]
        + (
            [
                pltpu.VMEM(full_out_shape, BF16),
                sems(()),
                sems(()),
                sems((len(out_pieces), peers - 1)),
                sems((len(out_pieces), peers - 1)),
            ]
            if ring_out
            else []
        ),
        compiler_params=pltpu.CompilerParams(
            collective_id=0, has_side_effects=True, vmem_limit_bytes=60 * 1024 * 1024
        ),
        name="gather_start",
    )(small, chunk, layer_input, cotangent, out_rows)


def ring_stream(peers, place, following, preceding, grad, slots, rows, first, size, way, sends, recvs):
    def local(step):
        owner = ring_shard(place - way * (1 + step), peers)
        return grad.at[pl.ds(pl.multiple_of(owner * rows + first, 8), size)]

    def copy(step):
        return remote(
            local(0) if step == 0 else slots.at[step - 1],
            slots.at[step],
            sends.at[step],
            recvs.at[step],
            {"shard": following if way > 0 else preceding},
        )

    def send(step):
        if step:
            copy(step - 1).wait_recv()
            slots[step - 1] = slots[step - 1] + local(step)[...]
        copy(step).start()

    def finish(target):
        copy(peers - 2).wait_recv()
        target[pl.ds(first, size), :] = slots[peers - 2] + local(peers - 1)[...]

    def drain():
        for step in range(peers - 1):
            copy(step).wait_send()

    return send, finish, drain


class Fold:
    tile = 256

    def __init__(self, product, tokens, give, got, far_out, far_in, total, sems):
        self.product, self.tokens = product, tokens
        self.give, self.got, self.far_out, self.far_in, self.total = give, got, far_out, far_in, total
        self.near_send, self.near_recv, self.far_send, self.far_recv = sems
        peers = lax.axis_size("head")
        mine = lax.axis_index("head")
        self.chips = peers // 2
        self.chip, self.core = lax.div(mine, 2), lax.rem(mine, 2)
        self.sibling, self.there, _ = head_peers()

    def near(self, by):
        return remote(
            self.give, self.got.at[by], self.near_send.at[by], self.near_recv.at[by], {"head": self.sibling}
        )

    def far(self, by):
        return remote(
            self.far_out.at[by - 1], self.far_in.at[by - 1], self.far_send.at[by - 1], self.far_recv.at[by - 1],
            {"head": self.there[by - 1]},
        )

    def rows(self, by, core, write):
        owner = lax.rem(self.chip + by, self.chips) * 2 + core

        def step(i, carry):
            here = pl.multiple_of(i * self.tile, self.tile)
            write(pl.ds(here, self.tile), self.product(pl.multiple_of(owner * self.tokens + here, self.tile), self.tile))
            return carry

        lax.fori_loop(0, self.tokens // self.tile, step, 0)

    def tasks(self):
        order = list(range(1, self.chips)) + [0]
        tasks = []
        for number, by in enumerate(order):

            def hand(by=by, before=order[number - 1] if number else None):
                if before is not None:
                    self.near(before).wait_send()

                def write(at, value):
                    self.give[at, :] = value

                self.rows(by, 1 - self.core, write)
                self.near(by).start()

            tasks.append(hand)
        for by in order:

            def keep(by=by):
                self.near(by).wait_recv()

                def write(at, value):
                    value = value + self.got[by, at, :]
                    if by:
                        self.far_out[by - 1, at, :] = value.astype(BF16)
                    else:
                        self.total[at, :] = value

                self.rows(by, self.core, write)
                if by:
                    self.far(by).start()

            tasks.append(keep)
        return tasks

    def arrive(self):
        for by in range(1, self.chips):
            self.far(by).wait_recv()

    def whole(self, at):
        value = self.total[at, :]
        for by in range(1, self.chips):
            value = value + self.far_in[by - 1, at, :].astype(F32)
        return value

    def drain(self):
        self.near(0).wait_send()
        for by in range(1, self.chips):
            self.far(by).wait_send()


def fold_scratch(tokens):
    chips = lax.axis_size("head") // 2
    sems = pltpu.SemaphoreType.DMA
    return [
        pltpu.VMEM((tokens, D), F32),
        pltpu.VMEM((chips, tokens, D), F32),
        pltpu.VMEM((chips - 1, tokens, D), BF16),
        pltpu.VMEM((chips - 1, tokens, D), BF16),
        sems((chips,)),
        sems((chips,)),
        sems((chips - 1,)),
        sems((chips - 1,)),
    ]


def ring_chain_kernel(
    gate_pieces, out_pieces, gate_ref, out_ref, own_ref, decay_ref, mixed_ref, full_ref, input_ref,
    part_gate_ref, part_out_ref, after_ref, result_ref,
    gate_slots, out_slots, outbox, inbox, gate_send, gate_recv, out_send, out_recv, chain_send, chain_recv,
    give, got, far_out, far_in, near_sends, near_recvs, far_sends, far_recvs,
):
    peers = lax.axis_size("shard")
    shard = lax.axis_index("shard")
    sibling, there, _ = head_peers()
    place = ring_position(shard, peers)
    following, preceding = ring_shard(place + 1, peers), ring_shard(place - 1, peers)
    barrier = greet(
        [{"shard": following}, {"shard": preceding}, {"head": sibling}]
        + [{"head": other} for other in there]
    )

    @pl.when(shard < peers - 1)
    def _():
        pl.semaphore_signal(barrier, inc=1, device_id={"shard": shard + 1}, device_id_type=MESH)

    @pl.when(shard > 0)
    def _():
        pl.semaphore_wait(barrier, 4 + len(there))

    @pl.when(shard == 0)
    def _():
        pl.semaphore_wait(barrier, 3 + len(there))

    streams = []
    for cuts, grad, slots, part, sends, recvs in (
        (gate_pieces, gate_ref, gate_slots, part_gate_ref, gate_send, gate_recv),
        (out_pieces, out_ref, out_slots, part_out_ref, out_send, out_recv),
    ):
        for number, (first, size, way) in enumerate(cuts):
            stream = ring_stream(
                peers, place, following, preceding, grad, slots.at[number],
                part.shape[0], first, size, way, sends.at[number], recvs.at[number],
            )
            streams.append((*stream, part))

    def product(row, rows):
        return contract(mixed_ref[pl.ds(row, rows), :], full_ref[...], NN)

    fold = Fold(
        product, input_ref.shape[0], give, got, far_out, far_in, result_ref,
        (near_sends, near_recvs, far_sends, far_recvs),
    )
    tasks = fold.tasks()

    turn = peers - 1 - shard
    chain_copy = remote(outbox, inbox, chain_send, chain_recv, {"shard": lax.rem(shard + peers - 1, peers)})

    def chain_step(step):
        @pl.when(turn == step)
        def _():
            if step == 0:
                after_ref[...] = jnp.zeros_like(after_ref)
            else:
                chain_copy.wait_recv()
                after_ref[...] = inbox[...]
            if step < peers - 1:
                outbox[...] = after_ref[...] * decay_ref[0:1, :] + own_ref[...]
                chain_copy.start()

    for step in range(peers - 1):
        for send, _, _, _ in streams:
            send(step)
        chain_step(step)
        if step < len(tasks):
            tasks[step]()
    chain_step(peers - 1)
    for task in tasks[peers - 1 :]:
        task()
    for _, finish, _, part in streams:
        finish(part)
    fold.arrive()
    for start in range(0, input_ref.shape[0], Fold.tile):
        at = pl.ds(start, Fold.tile)
        result_ref[at, :] = input_ref[at, :] + fold.whole(at)
    fold.drain()
    for _, _, drain, _ in streams:
        drain()

    @pl.when(shard > 0)
    def _():
        chain_copy.wait_send()


def slots_of(pieces, peers, cols):
    sizes = {size for _, size, _ in pieces}
    return pltpu.VMEM((len(pieces), peers - 1, max(sizes), cols), F32)


def even_pieces(rows):
    pieces = cut_rows(rows, 8)
    if len({size for _, size, _ in pieces}) > 1:
        step = 8
        pieces = [
            (start, step, 1 if number % 2 == 0 else -1)
            for number, start in enumerate(range(0, rows, step))
        ]
    return pieces


def ring_chain(grad_gate, grad_out, own, decay, mixed, full_out, layer_input):
    peers = lax.axis_size("shard")
    gate_pieces = even_pieces(grad_gate.shape[0] // peers)
    out_pieces = even_pieces(grad_out.shape[0] // peers)
    inside = pl.BlockSpec(memory_space=pltpu.VMEM)
    sems = pltpu.SemaphoreType.DMA
    return pl.pallas_call(
        functools.partial(ring_chain_kernel, gate_pieces, out_pieces),
        out_shape=[
            jax.ShapeDtypeStruct((grad_gate.shape[0] // peers, grad_gate.shape[1]), F32),
            jax.ShapeDtypeStruct((grad_out.shape[0] // peers, grad_out.shape[1]), F32),
            jax.ShapeDtypeStruct(own.shape, F32),
            jax.ShapeDtypeStruct(layer_input.shape, F32),
        ],
        in_specs=[inside] * 7,
        out_specs=[inside] * 4,
        scratch_shapes=[
            slots_of(gate_pieces, peers, grad_gate.shape[1]),
            slots_of(out_pieces, peers, grad_out.shape[1]),
            pltpu.VMEM(own.shape, F32),
            pltpu.VMEM(own.shape, F32),
            sems((len(gate_pieces), peers - 1)),
            sems((len(gate_pieces), peers - 1)),
            sems((len(out_pieces), peers - 1)),
            sems((len(out_pieces), peers - 1)),
            sems(()),
            sems(()),
        ]
        + fold_scratch(layer_input.shape[0]),
        compiler_params=pltpu.CompilerParams(
            collective_id=2, has_side_effects=True, vmem_limit_bytes=60 * 1024 * 1024
        ),
        name="ring_gate_out",
    )(grad_gate, grad_out, own, decay, mixed, full_out, layer_input)


def ring_rest_kernel(
    pieces, grad_ref, gate_ref, rest_ref, full_ref, input_ref, cot_ref, gain_ref, small_ref,
    part_gate_ref, part_out_ref, all_ref, dinput_ref, small_out_ref, all_gate_ref, all_out_ref,
    slots, part, ring_send, ring_recv, out_send, out_recv, next_send, next_recv, local_sems,
    small_in, gain_mine, gain_in, small_all, small_send, small_recv, gain_send, gain_recv, all_send, all_recv,
    out_piece, piece_send, piece_recv, gate_sems, out_sems, stay_sems,
    give, got, far_out, far_in, near_sends, near_recvs, far_sends, far_recvs,
):
    peers, heads = lax.axis_size("shard"), lax.axis_size("head")
    shard, head = lax.axis_index("shard"), lax.axis_index("head")
    sibling, there, source = head_peers()
    place = ring_position(shard, peers)
    following, preceding = ring_shard(place + 1, peers), ring_shard(place - 1, peers)
    shards = [lax.rem(shard + by, peers) for by in range(1, peers)]
    mates = [lax.rem(head + by, heads) for by in range(1, heads)]
    barrier = greet([{"shard": other} for other in shards] + [{"head": other} for other in mates])
    stored_by, worked_by, at_home = home_of(head, shard, heads, peers)
    greet_across(barrier, worked_by, at_home, len(shards) + len(mates))
    piece_copy = remote(part_out_ref, out_piece, piece_send, piece_recv, stored_by)
    gate_gather = HeadGather(part_gate_ref, all_gate_ref, [gate_sems.at[i] for i in range(4)])
    out_gather = HeadGather(out_piece, all_out_ref, [out_sems.at[i] for i in range(4)])
    stays = [
        pltpu.make_async_copy(part_gate_ref, gate_gather.at(head), stay_sems.at[0]),
        pltpu.make_async_copy(out_piece, out_gather.at(head), stay_sems.at[1]),
    ]
    rows = part.shape[0]
    tokens = input_ref.shape[0]
    small_rows = small_ref.shape[1]
    streams = [
        ring_stream(
            peers, place, following, preceding, grad_ref, slots.at[number],
            rows, first, size, way, ring_send.at[number], ring_recv.at[number],
        )
        for number, (first, size, way) in enumerate(pieces)
    ]
    gate_width, rest_width = gate_ref.shape[1], rest_ref.shape[1]

    def product(row, count):
        at = pl.ds(row, count)
        return contract(gate_ref[at, :], full_ref[:, 0:gate_width], NT) + contract(
            rest_ref[at, :], full_ref[:, gate_width : gate_width + rest_width], NT
        )

    fold = Fold(
        product, tokens, give, got, far_out, far_in, dinput_ref,
        (near_sends, near_recvs, far_sends, far_recvs),
    )
    tasks = fold.tasks()
    small_copies = [
        remote(
            small_ref.at[shards[by]], small_in.at[by], small_send.at[by], small_recv.at[by], {"shard": shards[by]}
        )
        for by in range(peers - 1)
    ]
    for step in range(peers - 1):
        for send, _, _ in streams:
            send(step)
        if step == 0:
            for copy in small_copies:
                copy.start()

            @pl.when(jnp.logical_not(at_home))
            def _():
                piece_copy.start()

            @pl.when(at_home)
            def _():
                out_piece[...] = part_out_ref[...]

            gate_gather.start()
            stays[0].start()
        if step == 2:

            @pl.when(jnp.logical_not(at_home))
            def _():
                piece_copy.wait()

            gate_gather.pass_on()
            out_gather.start()
            stays[1].start()
        if step == 4:
            out_gather.pass_on()
        if step < len(tasks):
            tasks[step]()
    for task in tasks[peers - 1 :]:
        task()

    def at_rows(owner, first, size):
        return pl.ds(pl.multiple_of(owner * rows + first, 8), size)

    waits, far = [], []
    for number, (first, size, _) in enumerate(pieces):
        streams[number][1](part)
        mine = part.at[pl.ds(first, size)]
        target = all_ref.at[at_rows(head, first, size)]
        for by in range(len(there)):
            copy = remote(mine, target, out_send.at[number, by], out_recv.at[number, by], {"head": there[by]})
            copy.start()
            far.append((number, by, copy))
        copy = remote(mine, target, next_send.at[number, 0], next_recv.at[number, 0], {"head": sibling})
        copy.start()
        waits.append(copy)
        copy = pltpu.make_async_copy(mine, target, local_sems.at[number])
        copy.start()
        waits.append(copy)

    fold.arrive()
    gain = gain_ref[0:1, :]
    gain_sum = jnp.zeros((8, D), F32)
    for start in range(0, tokens, Fold.tile):
        at = pl.ds(start, Fold.tile)
        d_normed = fold.whole(at)
        value = input_ref[at, :]
        scale = lax.rsqrt(jnp.mean(value * value, axis=-1, keepdims=True) + EPSILON)
        unit = value * scale
        product_rows = d_normed * unit
        for group in range(0, Fold.tile, 8):
            gain_sum = gain_sum + product_rows[group : group + 8, :]
        d_hat = d_normed * gain
        dinput_ref[at, :] = cot_ref[at, :] + scale * (
            d_hat - unit * jnp.mean(d_hat * unit, axis=-1, keepdims=True)
        )
    gain_row = jnp.sum(gain_sum, axis=0, keepdims=True)
    gain_mine[...] = jnp.concatenate(
        [gain_row[:, start : start + LANES] for start in range(0, D, LANES)]
        + [jnp.zeros((16 - D // LANES, LANES), F32)],
        axis=0,
    )
    gain_copies = [
        remote(gain_mine, gain_in.at[by], gain_send.at[by], gain_recv.at[by], {"shard": shards[by]})
        for by in range(peers - 1)
    ]
    for copy in gain_copies:
        copy.start()
    for number, by, copy in far:
        first, size, _ = pieces[number]
        copy.wait_recv()
        landed = all_ref.at[at_rows(source[by], first, size)]
        onward = remote(
            landed, landed, next_send.at[number, 1 + by], next_recv.at[number, 1 + by], {"head": sibling}
        )
        onward.start()
        waits.append(onward)

    small = small_ref[pl.ds(shard, 1)][0]
    gains = gain_mine[...]
    for copy in small_copies + gain_copies:
        copy.wait_recv()
    for by in range(peers - 1):
        small = small + small_in[by]
        gains = gains + gain_in[by]
    small_all[pl.ds(head, 1), 0:small_rows, :] = small[None]
    small_all[pl.ds(head, 1), small_rows:, :] = gains[None]
    all_copies = [
        remote(
            small_all.at[head], small_all.at[head], all_send.at[by], all_recv.at[by], {"head": mates[by]}
        )
        for by in range(heads - 1)
    ]
    for copy in all_copies:
        copy.start()
    for copy in all_copies:
        copy.wait_recv()
    everything = small_all[0]
    for other in range(1, heads):
        everything = everything + small_all[other]
    small_out_ref[...] = everything

    for gather in (gate_gather, out_gather):
        gather.finish()
        gather.drain()
    for copy in waits + stays:
        copy.wait()
    for _, _, copy in far:
        copy.wait_send()
    for copy in small_copies + gain_copies + all_copies:
        copy.wait_send()
    fold.drain()
    for _, _, drain in streams:
        drain()


def ring_rest(grad, d_gate, d_rest, full_in, layer_input, cotangent, gain, small, part_gate, part_out):
    peers, heads = lax.axis_size("shard"), lax.axis_size("head")
    chips = heads // 2
    rows, cols = grad.shape[0] // peers, grad.shape[1]
    pieces = even_pieces(rows)
    count = len(pieces)
    small_rows = small.shape[1]
    sems = pltpu.SemaphoreType.DMA
    inside = pl.BlockSpec(memory_space=pltpu.VMEM)
    outside = pl.BlockSpec(memory_space=pl.ANY)
    return pl.pallas_call(
        functools.partial(ring_rest_kernel, pieces),
        out_shape=[
            jax.ShapeDtypeStruct((heads * rows, cols), F32),
            jax.ShapeDtypeStruct(layer_input.shape, F32),
            jax.ShapeDtypeStruct((small_rows + 16, LANES), F32),
            jax.ShapeDtypeStruct((heads * part_gate.shape[0], part_gate.shape[1]), F32),
            jax.ShapeDtypeStruct((heads * part_out.shape[0], part_out.shape[1]), F32),
        ],
        in_specs=[inside] * 10,
        out_specs=[outside, inside, inside, outside, outside],
        scratch_shapes=[
            slots_of(pieces, peers, cols),
            pltpu.VMEM((rows, cols), F32),
            sems((count, peers - 1)),
            sems((count, peers - 1)),
            sems((count, max(chips - 1, 1))),
            sems((count, max(chips - 1, 1))),
            sems((count, chips)),
            sems((count, chips)),
            sems((count,)),
            pltpu.VMEM((peers - 1, small_rows, LANES), F32),
            pltpu.VMEM((16, LANES), F32),
            pltpu.VMEM((peers - 1, 16, LANES), F32),
            pltpu.VMEM((heads, small_rows + 16, LANES), F32),
            sems((peers - 1,)),
            sems((peers - 1,)),
            sems((peers - 1,)),
            sems((peers - 1,)),
            sems((heads - 1,)),
            sems((heads - 1,)),
            pltpu.VMEM(part_out.shape, F32),
            sems(()),
            sems(()),
            sems((4, chips)),
            sems((4, chips)),
            sems((2,)),
        ]
        + fold_scratch(layer_input.shape[0]),
        compiler_params=pltpu.CompilerParams(
            collective_id=3, has_side_effects=True, vmem_limit_bytes=60 * 1024 * 1024
        ),
        name="ring_rest",
    )(grad, d_gate, d_rest, full_in, layer_input, cotangent, gain, small, part_gate, part_out)


def exchange_kernel(
    width, own_bc, rest_in_ref, bc_ref, first_ref, tail_ref, taps_ref, rest_ref,
    after, sent, got, apart, misc, edge, edge_send, edge_recv, near_send, near_recv, far_send, far_recv, local_sems,
):
    peers = lax.axis_size("shard")
    shard, head = lax.axis_index("shard"), lax.axis_index("head")
    sibling, there, _ = head_peers()
    chips = lax.axis_size("head") // 2
    chip, core = lax.div(head, 2), lax.rem(head, 2)
    tokens = bc_ref.shape[1]
    following, preceding = lax.rem(shard + 1, peers), lax.rem(shard + peers - 1, peers)
    barrier = greet(
        [{"shard": following}, {"head": sibling}] + [{"head": other} for other in there]
    )
    pl.semaphore_wait(barrier, 2 + len(there))
    edge_copy = remote(first_ref, after, edge_send, edge_recv, {"shard": preceding})
    edge_copy.start()
    read = pltpu.make_async_copy(rest_ref.at[:, pl.ds(width, LANES)], misc, local_sems.at[0])
    read.start()
    edge_copy.wait_recv()
    nearer = jnp.where(shard < peers - 1, 1.0, 0.0)
    reach_back = jnp.zeros((16, first_ref.shape[1]), F32)
    for tap in range(CONV - 1):
        reach = CONV - 1 - tap
        reach_back = reach_back + jnp.concatenate(
            [
                jnp.zeros((16 - reach, first_ref.shape[1]), F32),
                taps_ref[tap : tap + 1, :] * after[0:reach, :] * nearer,
            ],
            axis=0,
        )
    edge[...] = (tail_ref[:, 0:width] + reach_back[:, 0:width]).astype(BF16)
    write_edge = pltpu.make_async_copy(
        edge, rest_ref.at[pl.ds(tokens - 16, 16), pl.ds(0, width)], local_sems.at[1]
    )
    write_edge.start()
    last = slice(tokens - LANES, tokens)
    turned = [
        jnp.transpose(
            jnp.concatenate(
                [
                    jnp.zeros((LANES - 16, NSTATE), F32),
                    reach_back[:, width + part * NSTATE : width + (part + 1) * NSTATE],
                ],
                axis=0,
            )
        )
        for part in range(2)
    ]
    is_second = core == 1
    sent[...] = jnp.where(is_second, bc_ref[0:NSTATE, :], bc_ref[NSTATE:, :])
    sent[:, last] = sent[:, last] + jnp.where(is_second, turned[0], turned[1])
    near = remote(sent, got, near_send, near_recv, {"head": sibling})
    near.start()
    near.wait_recv()
    got[...] = got[...] + jnp.where(is_second, bc_ref[NSTATE:, :], bc_ref[0:NSTATE, :])
    got[:, last] = got[:, last] + jnp.where(is_second, turned[1], turned[0])
    far = []
    for by in range(1, chips):
        theirs = pl.ds(pl.multiple_of(lax.rem(chip + by, chips) * own_bc, 8), own_bc)
        far.append(
            remote(
                got.at[theirs], apart.at[by - 1], far_send.at[by - 1], far_recv.at[by - 1],
                {"head": there[by - 1]},
            )
        )
        far[-1].start()
    read.wait()
    for copy in far:
        copy.wait_recv()
    mine = pl.ds(pl.multiple_of(chip * own_bc, 8), own_bc)
    lane_id = lax.broadcasted_iota(jnp.int32, (BLOCK, LANES), 1)
    for start in range(0, tokens, BLOCK):
        cols = slice(start, start + BLOCK)
        share = got[mine, cols]
        for by in range(1, chips):
            share = share + apart[by - 1, :, cols]
        share = jnp.transpose(
            jnp.concatenate([share, jnp.zeros((LANES - own_bc, BLOCK), F32)], axis=0)
        )
        misc[cols, :] = jnp.where(lane_id < own_bc, share, misc[cols, :].astype(F32)).astype(BF16)
    write = pltpu.make_async_copy(misc, rest_ref.at[:, pl.ds(width, LANES)], local_sems.at[2])
    write.start()
    write.wait()
    write_edge.wait()
    edge_copy.wait_send()
    near.wait_send()
    for copy in far:
        copy.wait_send()


def exchange(d_rest, d_bc, first, tail, taps, width, own_bc):
    chips = lax.axis_size("head") // 2
    tokens = d_rest.shape[0]
    sems = pltpu.SemaphoreType.DMA
    inside = pl.BlockSpec(memory_space=pltpu.VMEM)
    outside = pl.BlockSpec(memory_space=pl.ANY)
    return pl.pallas_call(
        functools.partial(exchange_kernel, width, own_bc),
        out_shape=jax.ShapeDtypeStruct(d_rest.shape, d_rest.dtype),
        in_specs=[outside] + [inside] * 4,
        out_specs=outside,
        input_output_aliases={0: 0},
        scratch_shapes=[
            pltpu.VMEM(first.shape, F32),
            pltpu.VMEM((NSTATE, tokens), F32),
            pltpu.VMEM((NSTATE, tokens), F32),
            pltpu.VMEM((chips - 1, own_bc, tokens), F32),
            pltpu.VMEM((tokens, LANES), BF16),
            pltpu.VMEM((16, width), BF16),
            sems(()),
            sems(()),
            sems(()),
            sems(()),
            sems((chips - 1,)),
            sems((chips - 1,)),
            sems((3,)),
        ],
        compiler_params=pltpu.CompilerParams(
            collective_id=4, has_side_effects=True, vmem_limit_bytes=VMEM_LIMIT
        ),
        name="exchange",
    )(d_rest, d_bc, first, tail, taps)


UPDATE_ROWS = 24


def update_kernel(
    own_bc, local_heads, gate_ref, rest_ref, out_ref, win_ref, fin_ref, sin_ref, wout_ref, fout_ref, sout_ref,
    one_in_ref, two_in_ref, new_in_ref, one_out_ref, two_out_ref, new_out_ref,
):
    heads, _, width = gate_ref.shape

    def step(refs, cols, gradient):
        weight, first, second, one, two, new = refs
        one[:, cols], two[:, cols], new[:, cols] = adamw(
            weight[:, cols], first[:, cols], second[:, cols], gradient, RATE_MATRIX, DECAY_MATRIX
        )

    into = (win_ref, fin_ref, sin_ref, one_in_ref, two_in_ref, new_in_ref)
    for head in range(heads):
        step(into, slice(head * width, (head + 1) * width), gate_ref[head])
        step(into, slice(DI + head * width, DI + (head + 1) * width), rest_ref[head, :, 0:width])
    order = [chip * 2 + core for core in range(2) for chip in range(heads // 2)]
    tail = [rest_ref[head, :, width : width + own_bc] for head in order] + [
        rest_ref[head, :, width + own_bc : width + own_bc + local_heads] for head in range(heads)
    ]
    step(into, slice(2 * DI, 2 * DI + 2 * NSTATE + HEADS), jnp.concatenate(tail, axis=1))
    out = (wout_ref, fout_ref, sout_ref, one_out_ref, two_out_ref, new_out_ref)
    step(out, slice(0, D), out_ref[...])


def update(all_gate, all_rest, all_out, into, out, own_bc, local_heads):
    heads = lax.axis_size("head")
    rows, cols = into[0].shape
    steps = rows // UPDATE_ROWS
    out_rows = out[0].shape[0] // steps
    whole = lambda i: (0, i, 0)
    flat = lambda i: (i, 0)
    all_gate = all_gate.reshape(heads, rows, -1)
    all_rest = all_rest.reshape(heads, rows, -1)
    in_block, out_block = (UPDATE_ROWS, cols), (out_rows, D)
    return blocked(
        functools.partial(update_kernel, own_bc, local_heads),
        "update",
        steps,
        [
            (all_gate, (heads, UPDATE_ROWS, all_gate.shape[2]), whole),
            (all_rest, (heads, UPDATE_ROWS, all_rest.shape[2]), whole),
            (all_out, out_block, flat),
        ]
        + [(array, in_block, flat) for array in into]
        + [(array, out_block, flat) for array in out],
        [(into[0].shape, F32, in_block, flat)] * 3 + [(out[0].shape, F32, out_block, flat)] * 3,
        [],
        10**8,
        5 * 10**7,
    )


def row_owner_pairs(head_count, shard_count):
    pairs = []
    for stored in range(shard_count):
        for slot in range(head_count):
            piece = stored * head_count + slot
            head, shard = piece // shard_count, piece % shard_count
            pairs.append((slot * shard_count + stored, head * shard_count + shard))
    return pairs


def per_device(
    layer_input,
    cotangent,
    weight_in,
    first_in,
    second_in,
    weight_out,
    first_out,
    second_out,
    small_params,
    first_small,
    second_small,
):
    head_count = lax.axis_size("head")
    shard_count = lax.axis_size("shard")
    tok_rows = layer_input.shape[0]
    group_rows = head_count * tok_rows
    local_heads = HEADS // head_count
    head_width = DI // head_count
    block_count = group_rows // BLOCK
    own_bc = 2 * NSTATE // head_count
    head_index = lax.axis_index("head")
    shard_index = lax.axis_index("shard")
    chip_index, core_index = head_index // 2, head_index % 2
    chan_start = head_index * head_width
    head_start = head_index * local_heads
    bc_start = core_index * NSTATE + chip_index * own_bc

    misc = LANES
    columns = [
        lax.dynamic_slice_in_dim(weight_in, chan_start, head_width, 1),
        lax.dynamic_slice_in_dim(weight_in, DI + chan_start, head_width, 1),
        lax.dynamic_slice_in_dim(weight_in, 2 * DI + bc_start, own_bc, 1),
        lax.dynamic_slice_in_dim(weight_in, DI + XBC + head_start, local_heads, 1),
        jnp.zeros((weight_in.shape[0], misc - own_bc - local_heads), F32),
        weight_in[:, 2 * DI : DI + XBC],
    ]
    at_x, at_misc, at_bc = head_width, 2 * head_width, 2 * head_width + misc
    at_dt = at_misc + own_bc
    small_low = small_params.astype(BF16)
    own_small = small_low.shape[0]
    flat = lax.dynamic_update_slice_in_dim(
        jnp.zeros((own_small * shard_count,), BF16), small_low, shard_index * own_small, 0
    )
    small_block = jnp.concatenate(
        [
            jnp.pad(small_low, (0, SMALL_ROWS * LANES - own_small)).reshape(SMALL_ROWS, LANES),
            jnp.pad(flat[-D:].reshape(D // LANES, LANES), ((0, 16 - D // LANES), (0, 0))),
        ],
        axis=0,
    )
    piece_rows = weight_out.shape[0] // head_count
    chunk = jnp.concatenate(columns, axis=1).astype(BF16)
    out_piece = lax.dynamic_slice_in_dim(weight_out, head_index * piece_rows, piece_rows, 0).astype(BF16)
    full_in, normed, cot_low, projected, smalls, before, *full_out = gather_start(
        small_block, chunk, layer_input, cotangent, out_piece
    )
    if full_out:
        (full_out,) = full_out
    else:
        pairs = row_owner_pairs(head_count, shard_count)
        out_piece = lax.ppermute(out_piece, ("head", "shard"), pairs)
        full_out = lax.all_gather(out_piece, "shard", axis=0, tiled=True)
    full_small = smalls[:, :SMALL_ROWS].reshape(shard_count, -1)[:, :own_small].reshape(-1)
    conv_weight, conv_bias, dt_bias, a_log, skip_all, norm_all, pre_gain = unpack(
        full_small.astype(F32)
    )
    d_mixed = jnp.einsum("td,id->ti", cot_low, full_out, preferred_element_type=F32)

    width, span = head_width, head_width + 2 * NSTATE
    taps = jnp.concatenate(
        [
            jnp.concatenate(
                [lax.dynamic_slice_in_dim(conv_weight, chan_start, width, 1), conv_weight[:, DI:]], 1
            ),
            jnp.concatenate(
                [lax.dynamic_slice_in_dim(conv_bias, chan_start, width, 0), conv_bias[DI:]]
            )[None],
            jnp.zeros((8 - CONV - 1, span), F32),
        ],
        axis=0,
    )
    decay_rate = -jnp.exp(lax.dynamic_slice_in_dim(a_log, head_start, local_heads))
    offset_heads = lax.dynamic_slice_in_dim(dt_bias, head_start, local_heads)
    skip_gain = lax.dynamic_slice_in_dim(skip_all, head_start, local_heads)
    norm_gain = lax.dynamic_slice_in_dim(norm_all, chan_start, width, 0)
    lanes = (own_bc, LANES - own_bc - local_heads)
    heads = jnp.pad(jnp.stack([offset_heads, decay_rate]), ((0, 6), lanes))
    chans = jnp.pad(jnp.stack([jnp.repeat(skip_gain, HEADDIM), norm_gain]), ((0, 6), (0, 0)))

    steps = block_count
    at_b = at_bc // LANES
    misc_at = at_misc // LANES
    ahead = lambda col: (lambda i: (i, col))
    back = lambda col: (lambda i: (steps - 1 - i, col))
    fixed = lambda col: (lambda i: (0, col))
    last_rows = lambda col: (lambda i: (jnp.maximum((steps - 1 - i) * (BLOCK // 16) - 1, 0), col))
    rows = (BLOCK, width)
    lane_rows = (BLOCK, LANES)
    halo_in = [
        (before, (16, width), fixed(1)),
        (before, (16, LANES), fixed(at_b)),
        (before, (16, LANES), fixed(at_b + 1)),
    ]
    act, der, times, own_state, own_decay = blocked(
        functools.partial(prepare_kernel, own_bc),
        "conv_states",
        steps,
        [
            (projected, rows, ahead(1)),
            (projected, lane_rows, ahead(at_b)),
            (projected, lane_rows, ahead(at_b + 1)),
            (projected, lane_rows, ahead(misc_at)),
            *halo_in,
            (taps, (8, span), fixed(0)),
            (heads, (8, LANES), fixed(0)),
        ],
        [
            ((group_rows, span), F32, (BLOCK, span), ahead(0)),
            ((group_rows, span), F32, (BLOCK, span), ahead(0)),
            ((group_rows, 2 * LANES), F32, (BLOCK, 2 * LANES), ahead(0)),
            ((NSTATE, width), F32, (NSTATE, width), fixed(0)),
            ((8, width), F32, (8, width), fixed(0)),
        ],
        [pltpu.VMEM((BLOCK + 8, span), F32), pltpu.VMEM((8, LANES), F32)],
        10**10,
        4 * 10**7,
    )
    prior = chain(own_state, own_decay, 1)
    y_mix, y_ssm, sums, states, final = blocked(
        functools.partial(forward_kernel, own_bc),
        "scan_forward",
        steps,
        [
            (act, (BLOCK, span), ahead(0)),
            (times, (BLOCK, 2 * LANES), ahead(0)),
            (projected, rows, ahead(0)),
            (d_mixed, rows, ahead(0)),
            (chans, (8, width), fixed(0)),
            (prior, (NSTATE, width), fixed(0)),
        ],
        [
            ((group_rows, width), BF16, rows, ahead(0)),
            ((group_rows, width), F32, rows, ahead(0)),
            ((8, group_rows), F32, (8, BLOCK), lambda i: (0, i)),
            ((steps * NSTATE, width), F32, (NSTATE, width), ahead(0)),
            ((NSTATE, width), F32, (NSTATE, width), fixed(0)),
        ],
        [],
        2 * 10**10,
        5 * 10**7,
    )
    sums = sum_head(sums)
    mixed, d_gate, d_y, own_grad, gain_rows = blocked(
        functools.partial(gate_kernel, own_bc),
        "gated_norm",
        steps,
        [
            (act, lane_rows, back(span // LANES - 1)),
            (times, lane_rows, back(1)),
            (projected, rows, back(0)),
            (d_mixed, rows, back(0)),
            (y_mix, rows, back(0)),
            (sums, (8, BLOCK), lambda i: (0, steps - 1 - i)),
            (chans, (8, width), fixed(0)),
        ],
        [
            ((group_rows, width), BF16, rows, back(0)),
            ((group_rows, width), BF16, rows, back(0)),
            ((group_rows, width), F32, rows, back(0)),
            ((NSTATE, width), F32, (NSTATE, width), fixed(0)),
            ((8, width), F32, (8, width), fixed(0)),
        ],
        [],
        10**10,
        5 * 10**7,
    )
    grad_norm_gain = gain_rows[0]
    grad_out = jnp.einsum("ti,td->id", mixed, cot_low, preferred_element_type=F32)
    grad_gate = jnp.einsum("td,tf->df", normed, d_gate, preferred_element_type=F32)
    part_gate, part_out, after, result = ring_chain(
        grad_gate, grad_out, own_grad, own_decay, mixed, full_out, layer_input
    )
    d_rest, d_bc, first_conv, rest_raw, grad_taps, skip_rows, head_rows = blocked(
        functools.partial(backward_kernel, own_bc, local_heads),
        "scan_backward",
        steps,
        [
            (act, (BLOCK, span), back(0)),
            (der, (BLOCK, span), back(0)),
            (times, (BLOCK, 2 * LANES), back(0)),
            (d_y, rows, back(0)),
            (y_ssm, rows, back(0)),
            (states, (NSTATE, width), back(0)),
            (final, (NSTATE, width), fixed(0)),
            (after, (NSTATE, width), fixed(0)),
            (projected, lane_rows, back(misc_at)),
            (projected, rows, back(1)),
            (projected, lane_rows, back(at_b)),
            (projected, lane_rows, back(at_b + 1)),
            (projected, (16, width), last_rows(1)),
            (projected, (16, LANES), last_rows(at_b)),
            (projected, (16, LANES), last_rows(at_b + 1)),
            *halo_in,
            (taps, (8, span), fixed(0)),
            (heads, (8, LANES), fixed(0)),
            (chans, (8, width), fixed(0)),
        ],
        [
            ((group_rows, width + LANES), BF16, (BLOCK, width + LANES), back(0)),
            ((2 * NSTATE, group_rows), F32, (2 * NSTATE, BLOCK), lambda i: (0, steps - 1 - i)),
            ((8, span), F32, (8, span), fixed(0)),
            ((16, span), F32, (16, span), fixed(0)),
            ((8, span), F32, (8, span), fixed(0)),
            ((8, width), F32, (8, width), fixed(0)),
            ((8, LANES), F32, (8, LANES), fixed(0)),
        ],
        [
            pltpu.VMEM((NSTATE, width), F32),
            pltpu.VMEM((8, LANES), F32),
            pltpu.VMEM((BLOCK + 8, span), F32),
            pltpu.VMEM((BLOCK + 8, span), F32),
            pltpu.VMEM((BLOCK, width), F32),
        ],
        5 * 10**10,
        6 * 10**7,
    )
    grad_convw, grad_convb = grad_taps[:CONV], grad_taps[CONV]
    grad_skip = jnp.sum(skip_rows[0].reshape(local_heads, HEADDIM), axis=1)
    grad_dtb = head_rows[0, own_bc : own_bc + local_heads]
    grad_alog = head_rows[1, own_bc : own_bc + local_heads] * decay_rate

    d_rest = exchange(d_rest, d_bc, first_conv, rest_raw, taps, width, own_bc)
    grad_rest = jnp.einsum("td,tf->df", normed, d_rest, preferred_element_type=F32)

    def place(values, start, width):
        zeros = jnp.zeros(values.shape[:-1] + (width,), F32)
        return lax.dynamic_update_slice_in_dim(zeros, values, start, values.ndim - 1)

    conv_w_full = jnp.concatenate(
        [place(grad_convw[:, :head_width], chan_start, DI), grad_convw[:, head_width:]], axis=1
    ).reshape(-1)
    conv_b_full = jnp.concatenate(
        [place(grad_convb[:head_width], chan_start, DI), grad_convb[head_width:]]
    )
    grad_small = jnp.concatenate(
        [
            conv_w_full,
            conv_b_full,
            place(grad_dtb, head_start, HEADS),
            place(grad_alog, head_start, HEADS),
            place(grad_skip, head_start, HEADS),
            place(grad_norm_gain, chan_start, DI),
            jnp.zeros((D,), F32),
        ]
    )
    small_rows = 8 * (-(-own_small // (8 * LANES)))
    small_out = jnp.pad(
        grad_small.reshape(shard_count, own_small), ((0, 0), (0, small_rows * LANES - own_small))
    ).reshape(shard_count, small_rows, LANES)
    gain_in = jnp.broadcast_to(pre_gain, (8, D))
    all_rest, d_input, small_sums, all_gate, all_out = ring_rest(
        grad_rest, d_gate, d_rest, full_in, layer_input, cotangent, gain_in, small_out,
        part_gate, part_out,
    )
    gain_flat = jnp.concatenate(
        [
            jnp.zeros((own_small * shard_count - D,), F32),
            small_sums[small_rows : small_rows + D // LANES].reshape(D),
        ]
    )
    total_small = small_sums[:small_rows].reshape(-1)[:own_small] + lax.dynamic_slice_in_dim(
        gain_flat, shard_index * own_small, own_small
    )

    one_in, two_in, new_in, one_out, two_out, new_out = update(
        all_gate, all_rest, all_out,
        (weight_in, first_in, second_in), (weight_out, first_out, second_out),
        own_bc, local_heads,
    )
    one_small, two_small, new_small = adamw(
        small_params, first_small, second_small, total_small, RATE_SMALL, 0.0
    )
    return (
        result,
        d_input,
        one_in,
        two_in,
        new_in,
        one_out,
        two_out,
        new_out,
        one_small,
        two_small,
        new_small,
    )


def solution(mesh):
    rows = P(("shard", "head"), None)
    owned = P("shard", None)
    packed = P("shard")
    return jax.shard_map(
        per_device,
        mesh=mesh,
        in_specs=(rows, rows) + (owned,) * 6 + (packed,) * 3,
        out_specs=(rows, rows) + (owned,) * 6 + (packed,) * 3,
        check_vma=False,
    )
```

time: 2330 us -> 637 us (0.27)
  waiting for transfers between devices: 1490 us -> 3.54 us
  Pallas kernels: 0 us -> 551 us
  matrix products: 308 us -> 38.1 us
  other arithmetic: 181 us -> 2.61 us
  local copies, waits for them, and re-layouts: 181 us -> 28.8 us
  blocking collectives: 118 us -> 0 us
  starting transfers between devices: 28.5 us -> 1.97 us
    reduce_scatter x3 -> x0, waiting for transfers between devices: 799 us -> none  [the longest x1 643 us: per_device(): lax.psum_scatter(grad_in, 'shard', scatter_dimension=0, tiled=True)]
    pallas_call x0 -> x10, Pallas kernels: none -> 551 us  [the longest x5 137 us: blocked(): pl.pallas_call(kernel, grid=(steps,), in_specs=[pl.BlockSpec(block, index...]
    all_gather x5 -> x0, waiting for transfers between devices: 329 us -> none  [the longest x1 318 us: per_device(): lax.all_gather(weight_in.astype(jnp.bfloat16), 'shard', axis=0, tiled=True)]
    dot_general x22 -> x4, matrix products: 308 us -> 38.1 us  [the longest x1 11.7 us: per_device(): jnp.einsum('td,tf->df', normed, d_rest, preferred_element_type=F32)]
    all_to_all x6 -> x0, waiting for transfers between devices: 169 us -> none  [the longest x1 70.6 us: per_device(): lax.all_to_all(d_y.reshape(tok_rows, head_count, head_width), 'head', spl...]
    psum x1 -> x0, waiting for transfers between devices: 128 us -> none  [per_device(): lax.psum((part_in, part_out, part_small), 'head')]
    unnamed x1 -> x0, blocking collectives: 69.3 us -> none
    unnamed x11 -> x0, waiting for transfers between devices: 57.3 us -> none
  transfers between devices with their start and end apart: 18 -> 2, of which waited for: 12 -> 2; matrix products, arithmetic and copies ran while one was open for 18% -> 0% of each run, Pallas kernels for 0% -> 0%
where the time goes in v1:
time: 637 us; the launch traced here: 627 us
  Pallas kernels  551 us (86%)
  matrix products  38.1 us (6%)
  local copies, waits for them, and re-layouts  28.8 us (5%)
    pallas_call x5, Pallas kernels, blocked(): pl.pallas_call(kernel, grid=(steps,), in_specs=[pl.BlockSpec(block, index...  137 us
    pallas_call x1, Pallas kernels, gather_start(): pl.pallas_call(functools.partial(gather_kernel, ring_out, pieces, out_pie...  135 us
    pallas_call x1, Pallas kernels, ring_chain(): pl.pallas_call(functools.partial(ring_chain_kernel, gate_pieces, out_piec...  133 us
    pallas_call x1, Pallas kernels, ring_rest(): pl.pallas_call(functools.partial(ring_rest_kernel, pieces), out_shape=[ja...  118 us
    pallas_call x1, Pallas kernels, exchange(): pl.pallas_call(functools.partial(exchange_kernel, width, own_bc), out_sha...  17.4 us
    unnamed x48, local copies, waits for them, and re-layouts  16.7 us
  transfers between devices with their start and end apart: 2, of which 2 were waited for; matrix products, arithmetic and copies ran while one was open for 0% of the time, Pallas kernels for 0%

profile of v1, /device:TPU:0, one launch (start us, length us, event | category | flops | bytes accessed | tf_op | source)
XLA Modules:
  0.0 627.2 jit_solution(10119830721099120836)
XLA Ops:
  0.7 0.9 slice.142
  1.6 1.0 dynamic-slice_convert_fusion.4
  2.6 1.0 dynamic-slice_convert_fusion.3
  4.7 1.5 dynamic-slice_convert_fusion.1
  6.3 1.8 dynamic-slice_convert_fusion.out_ref
  8.7 1.0 concatenate.26.chunk_ref
  9.8 135.3 %gather_start.1 = (bf16[1536,1920]{1,0:T(8,128)(2,1)}, bf16[2048,1536]{1,0:T(8,128)(2,1)}, bf16[2048,1536]{1,0:T(8,128)(2,1)}, bf16[2048,1920]{1,0:T(8,128)(2,1)...) custom-call(bf16[48,128]{1,0:T(8,128)(2,1)} %fusion.2.small_ref, ...), custom_call_target="tpu_custom_call" | custom-call | tf_op jit(solution)/shard_map/gather_start/pallas_call | solution.py:865
  147.9 16.2 %conv_states.1 = (f32[2048,1024]{1,0:T(8,128)}, f32[2048,1024]{1,0:T(8,128)}, f32[2048,256]{1,0:T(8,128)S(1)}, f32[128,768]{1,0:T(8,128)S(1)}, f32[8,768]{1,0:T(8,128)S(1)}) custom-call(bf16[2048,1920]{1,0:T(8,128)(2,1)} %get-tuple-element.56.x_ref.b_ref.c_ref.misc_ref.gate_ref.px_ref.pb_ref.pc_ref, ...), custom_call_target="tpu_custom_call" | custom-call | flops 10000000000 | bytes 40000000 | tf_op jit(solution)/shard_map/conv_states/pallas_call | solution.py:528
  164.1 10.1 %carry_forward.1.prior_ref = f32[128,768]{1,0:T(8,128)S(1)} custom-call(f32[128,768]{1,0:T(8,128)S(1)} %get-tuple-element.63.own_ref, f32[8,768]{1,0:T(8,128)S(1)} %get-tuple-element.64.decay_ref), custom_call_target="tpu_custom_call" | custom-call | tf_op jit(solution)/shard_map/carry_forward/pallas_call | solution.py:507
  174.3 6.9 %fusion.10.dmix_ref = f32[2048,768]{1,0:T(8,128)} fusion(bf16[2048,1536]{1,0:T(8,128)(2,1)S(1)} %copy-done.20, bf16[768,1536]{1,0:T(8,128)(2,1)S(1)} %copy-done.16), kind=kOutput, calls=%fused_computation.47 | convolution fusion | flops 4831838208 | bytes 14942208 | tf_op jit(solution)/shard_map/td,id->ti/dot_general | solution.py:1681
  181.2 34.4 %scan_forward.1 = (bf16[2048,768]{1,0:T(8,128)(2,1)S(1)}, f32[2048,768]{1,0:T(8,128)}, f32[8,2048]{1,0:T(8,128)S(1)}, f32[1024,768]{1,0:T(8,128)}, f32[128,768]{1,0:T(8,128)S(1)}) custom-call(f32[2048,1024]{1,0:T(8,128)} %get-tuple-element.59.act_ref.c_ref, f32[2048,256]{1,0:T(8,128)S(1)} %get-tuple-element.60.time_ref, ...), custom_call_target="tpu_custom_call" | custom-call | flops 20000000000 | bytes 50000000 | tf_op jit(solution)/shard_map/scan_forward/pallas_call | solution.py:528
  215.6 1.7 copy-done.12
  217.3 1.9 collective-permute-start
  219.2 2.4 collective-permute-done
  221.7 1.2 collective-permute-done.1
  222.9 14.0 %gated_norm.1 = (bf16[2048,768]{1,0:T(8,128)(2,1)S(1)}, bf16[2048,768]{1,0:T(8,128)(2,1)}, f32[2048,768]{1,0:T(8,128)}, f32[128,768]{1,0:T(8,128)S(1)}, f32[8,768]{1,0:T(8,128)S(1)}) custom-call(f32[2048,1024]{1,0:T(8,128)} %get-tuple-element.59.act_ref.c_ref, f32[2048,256]{1,0:T(8,128)S(1)} %get-tuple-element.60.time_ref, ...), custom_call_target="tpu_custom_call" | custom-call | flops 10000000000 | bytes 50000000 | tf_op jit(solution)/shard_map/gated_norm/pallas_call | solution.py:528
  236.9 10.8 %fusion.12.out_ref = f32[768,1536]{1,0:T(8,128)} fusion(bf16[2048,768]{1,0:T(8,128)(2,1)S(1)} %get-tuple-element.68.mixed_ref, bf16[2048,1536]{1,0:T(8,128)(2,1)} %get-tuple-element.61), kind=kOutput, calls=%fused_computation.49 | convolution fusion | flops 4831838208 | bytes 14155776 | tf_op jit(solution)/shard_map/ti,td->id/dot_general | solution.py:1792
  247.8 8.7 %fusion.11.gate_ref = f32[1536,768]{1,0:T(8,128)} fusion(bf16[2048,1536]{1,0:T(8,128)(2,1)} %get-tuple-element.55, bf16[2048,768]{1,0:T(8,128)(2,1)S(1)} %copy-done.15), kind=kOutput, calls=%fused_computation.48 | convolution fusion | flops 4831838208 | bytes 14155776 | tf_op jit(solution)/shard_map/td,tf->df/dot_general | solution.py:1793
  256.4 132.9 %ring_gate_out.1 = (f32[192,768]{1,0:T(8,128)}, f32[96,1536]{1,0:T(8,128)}, f32[128,768]{1,0:T(8,128)}, f32[512,1536]{1,0:T(8,128)}) custom-call(f32[1536,768]{1,0:T(8,128)} %fusion.11.gate_ref, f32[768,1536]{1,0:T(8,128)} %fusion.12.out_ref, f32[128,768]{1,0:T(8,128)} %copy-done.5, f32[8,768]{1,0:T(8,128)} %copy-done.6, bf16[2048,768]{1,0:T(8,128)(2,1)} %copy-done.2, ...), custom_call_target="tpu_custom_call" | custom-call | tf_op jit(solution)/shard_map/ring_gate_out/pallas_call | solution.py:1155
  389.3 1.0 copy-done.7
  390.3 1.6 copy-done.11
  391.9 54.3 %scan_backward.1 = (bf16[2048,896]{1,0:T(8,128)(2,1)}, f32[256,2048]{1,0:T(8,128)S(1)}, f32[8,1024]{1,0:T(8,128)S(1)}, f32[16,1024]{1,0:T(8,128)S(1)}, f32[8,102...) custom-call(f32[2048,1024]{1,0:T(8,128)} %get-tuple-element.59.act_ref.c_ref, ...), custom_call_target="tpu_custom_call" | custom-call | flops 49999998976 | bytes 60000000 | tf_op jit(solution)/shard_map/scan_backward/pallas_call | solution.py:528
  448.8 2.0 copy-done
  450.8 17.4 %exchange.1.rest_ref = bf16[2048,896]{1,0:T(8,128)(2,1)S(1)} custom-call(bf16[2048,896]{1,0:T(8,128)(2,1)S(1)} %copy-done, f32[256,2048]{1,0:T(8,128)S(1)} %get-tuple-element.78.bc_ref, f32[8,1024]{1,0:T(8,128)S(1)} %get-tuple-element.79.first_ref, f32[16,1024]{1,0:T(8,128)S(1)} %get-tuple-element.80.tail_ref, ...), custom_call_target="tpu_custom_call", output_to_operand_aliasing={{}: (0, {})} | custom-call | tf_op jit(solution)/shard_map/exchange/pallas_call | solution.py:1520
  468.3 11.7 %fusion.13.grad_ref = f32[1536,896]{1,0:T(8,128)} fusion(bf16[2048,1536]{1,0:T(8,128)(2,1)} %get-tuple-element.55, bf16[2048,896]{1,0:T(8,128)(2,1)S(1)} %exchange.1.rest_ref), kind=kOutput, calls=%fused_computation.50 | convolution fusion | flops 5637144576 | bytes 15466496 | tf_op jit(solution)/shard_map/td,tf->df/dot_general | solution.py:1847
  480.6 118.3 %ring_rest.1 = (f32[768,896]{1,0:T(8,128)}, f32[512,1536]{1,0:T(8,128)}, f32[40,128]{1,0:T(8,128)}, f32[768,768]{1,0:T(8,128)}, f32[384,1536]{1,0:T(8,128)}) custom-call(f32[1536,896]{1,0:T(8,128)} %fusion.13.grad_ref, bf16[2048,768]{1,0:T(8,128)(2,1)} %get-tuple-element.67.gate_ref, bf16[2048,896]{1,0:T(8,128)(2,1)} %copy-done.1, ...), custom_call_target="tpu_custom_call" | custom-call | tf_op jit(solution)/shard_map/ring_rest/pallas_call | solution.py:1377
  601.1 1.7 copy-done.3
  602.8 1.7 copy-done.4
  604.4 17.9 %update.1 = (f32[192,6448]{1,0:T(8,128)}, f32[192,6448]{1,0:T(8,128)}, f32[192,6448]{1,0:T(8,128)}, f32[384,1536]{1,0:T(8,128)}, f32[384,1536]{1,0:T(8,128)}, /*index=5*/f32[384,1536]{1,0:T(8,128)}) custom-call(f32[4,192,768]{2,1,0:T(8,128)S(1)} %bitcast.40, f32[4,192,896]{2,1,0:T(8,128)} %bitcast.41, f32[384,1536]{1,0:T(8,128)S(1)} %copy-done.4, ...), custom_call_target="tpu_custom_call" | custom-call | flops 100000000 | bytes 50000000 | tf_op jit(solution)/shard_map/update/pallas_call | solution.py:528
  622.3 1.7 copy.40
  624.0 1.3 copy-done.14
  625.4 1.7 copy.41
  (101 shorter events, 9.9 us)
Async XLA Ops:
  147.0 0.8 copy-start.8
  147.9 26.4 %copy-start.16 = (bf16[768,1536]{1,0:T(8,128)(2,1)S(1)}, bf16[768,1536]{1,0:T(8,128)(2,1)}, u32[]{:S(2)}) copy-start(bf16[768,1536]{1,0:T(8,128)(2,1)} %get-tuple-element.62.full_ref) | copy-start | bytes 7077892
  147.9 26.4 %copy-start.20 = (bf16[2048,1536]{1,0:T(8,128)(2,1)S(1)}, bf16[2048,1536]{1,0:T(8,128)(2,1)}, u32[]{:S(2)}) copy-start(bf16[2048,1536]{1,0:T(8,128)(2,1)} %get-tuple-element.61) | copy-start | bytes 18874372
  164.1 17.1 %copy-start.6 = (f32[8,768]{1,0:T(8,128)}, f32[8,768]{1,0:T(8,128)S(1)}, u32[]{:S(2)}) copy-start(f32[8,768]{1,0:T(8,128)S(1)} %get-tuple-element.64.decay_ref) | copy-start | bytes 73732
  164.1 58.8 %copy-start.10 = (f32[2048,256]{1,0:T(8,128)}, f32[2048,256]{1,0:T(8,128)S(1)}, u32[]{:S(2)}) copy-start(f32[2048,256]{1,0:T(8,128)S(1)} %get-tuple-element.60.time_ref) | copy-start | bytes 6291460
  215.6 1.7 copy-start.12
  217.3 4.3 collective-permute-start
  221.5 1.3 collective-permute-start.1
  236.9 10.8 %copy-start.2 = (bf16[2048,768]{1,0:T(8,128)(2,1)}, bf16[2048,768]{1,0:T(8,128)(2,1)S(1)}, u32[]{:S(2)}) copy-start(bf16[2048,768]{1,0:T(8,128)(2,1)S(1)} %get-tuple-element.68.mixed_ref) | copy-start | bytes 9437188
  236.9 10.8 %copy-start.5 = (f32[128,768]{1,0:T(8,128)}, f32[128,768]{1,0:T(8,128)S(1)}, u32[]{:S(2)}) copy-start(f32[128,768]{1,0:T(8,128)S(1)} %get-tuple-element.69.own_ref) | copy-start | bytes 1179652
  236.9 10.8 %copy-start.15 = (bf16[2048,768]{1,0:T(8,128)(2,1)S(1)}, bf16[2048,768]{1,0:T(8,128)(2,1)}, u32[]{:S(2)}) copy-start(bf16[2048,768]{1,0:T(8,128)(2,1)} %get-tuple-element.67.gate_ref) | copy-start | bytes 9437188
  256.4 132.9 %copy-start.9 = (bf16[16,1920]{1,0:T(8,128)(2,1)S(1)}, bf16[16,1920]{1,0:T(8,128)(2,1)}, u32[]{:S(2)}) copy-start(bf16[16,1920]{1,0:T(8,128)(2,1)} %get-tuple-element.57.hx_ref.hb_ref.hc_ref) | copy-start | bytes 184324
  389.3 1.0 copy-start.7
  390.3 1.6 copy-start.11
  448.8 2.0 copy-start
  468.2 11.7 %copy-start.1 = (bf16[2048,896]{1,0:T(8,128)(2,1)}, bf16[2048,896]{1,0:T(8,128)(2,1)S(1)}, u32[]{:S(2)}) copy-start(bf16[2048,896]{1,0:T(8,128)(2,1)S(1)} %exchange.1.rest_ref) | copy-start | bytes 11010052
  480.6 119.8 %copy-start.17 = (f32[2674]{0:T(1024)S(1)}, f32[2674]{0:T(1024)}, u32[]{:S(2)}) copy-start(f32[2674]{0:T(1024)} %param.19) | copy-start | bytes 32092
  480.6 119.8 %copy-start.18 = (f32[2674]{0:T(1024)S(1)}, f32[2674]{0:T(1024)}, u32[]{:S(2)}) copy-start(f32[2674]{0:T(1024)} %param.21) | copy-start | bytes 32092
  480.6 119.8 %copy-start.19 = (f32[2674]{0:T(1024)S(1)}, f32[2674]{0:T(1024)}, u32[]{:S(2)}) copy-start(f32[2674]{0:T(1024)} %param.20) | copy-start | bytes 32092
  601.1 1.7 copy-start.3
  602.8 1.7 copy-start.4
  604.4 17.9 %copy-start.13 = (f32[512,1536]{1,0:T(8,128)S(1)}, f32[512,1536]{1,0:T(8,128)}, u32[]{:S(2)}) copy-start(f32[512,1536]{1,0:T(8,128)} %get-tuple-element.120) | copy-start | bytes 9437188
  622.3 3.0 copy-start.14
